TPU v7x, 512 devices: a whole 4x8x8 slice. The times are simulated.
512 devices in a mesh: blk: 128 (over y_hi, z, x, core), grp: 4 (over y_lo).
Axes of the slice: x: 4, y: 8 (y_hi: 2, y_lo: 4; y = y_hi * 4 + y_lo), z: 8, core: 2. Of those that a mesh axis runs over, the one named last changes fastest.
Arguments:
- amplitudes: bfloat16 [1024, 4, 8192], P(None, 'grp', 'blk'), may hold values from -6 to 6
- ladder_ints: bfloat16 [32768, 32768], P('grp', 'blk'), may hold values from -0.09375 to 0.09375
- pair_irrep: int32 [32768], replicated, may hold values from 0 to 7, as said below
- occ_gap: float32 [1024], replicated, may hold values from 0.5 to 3
- vir_energy: float32 [32768], P('blk'), may hold values from 0.5 to 5
- pair_subset: int32 [512], replicated, may hold values from 0 to 1023, as said below
Outputs:
- update: bfloat16 [512, 32768], P('grp', 'blk')
Inputs may be any that keep to these rules, and one draw needn't show every extreme that they name: `pair_subset`: the entries are distinct. `pair_irrep`: labels never fall along the pairs, so each irrep is one contiguous run of pairs, of uneven lengths; the first pair has label 0 and the last label 7.
All inputs are finite; a program needn't handle non-finite values.
Results may differ from a plain program's by a relative error of at most 0.001.
Values may be sent and summed in bfloat16 or wider, within the bound.
No kernel may reach another device: no remote copies, remote signals or barrier semaphores. Data moves between devices by JAX's collectives and lax.ppermute only.
A program may use at most 64 MiB of HBM per device.

v0:
```python
import jax
import jax.numpy as jnp
from jax import lax
from jax.sharding import PartitionSpec as P


def body(amplitudes, ladder_ints, pair_irrep, occ_gap, vir_energy, pair_subset):
    group_index = lax.axis_index("grp")
    block_index = lax.axis_index("blk")
    row_count = ladder_ints.shape[0]
    column_count = ladder_ints.shape[1]
    row_irrep = lax.dynamic_slice_in_dim(pair_irrep, group_index * row_count, row_count, 0)
    col_irrep = lax.dynamic_slice_in_dim(pair_irrep, block_index * column_count, column_count, 0)
    masked = jnp.where(
        row_irrep[:, None] == col_irrep[None, :], ladder_ints, jnp.zeros_like(ladder_ints)
    )
    chosen = jnp.take(amplitudes, pair_subset, axis=0)[:, 0, :]
    occ_count = chosen.shape[0]
    gathered = lax.all_gather(chosen, "blk", axis=1, tiled=True)
    ladder = jnp.dot(gathered, masked, preferred_element_type=jnp.float32)
    gaps = jnp.take(occ_gap, pair_subset)
    share_rows = occ_count // lax.axis_size("grp")
    owned = lax.psum_scatter(ladder, "grp", scatter_dimension=0, tiled=True)
    own_gaps = lax.dynamic_slice_in_dim(gaps, group_index * share_rows, share_rows, 0)
    return (owned / (own_gaps[:, None] + vir_energy[None, :])).astype(jnp.bfloat16)


def solution(mesh):
    return jax.shard_map(
        body,
        mesh=mesh,
        in_specs=(P(None, "grp", "blk"), P("grp", "blk"), P(), P(), P("blk"), P()),
        out_specs=P("grp", "blk"),
        check_vma=False,
    )
```

profile of v0, /device:TPU:1, one launch (start us, length us, event | category | flops | bytes accessed | tf_op | source)
XLA Modules:
  0.0 214.0 jit_solution(16848741103746112545)
XLA Ops:
  6.5 0.0 copy-start
  6.5 0.0 all-gather.2.cloned.1.call-start
  6.5 0.7 compare_select_fusion.2
  7.2 0.0 copy-done
  7.2 2.3 %gather_fusion.1 = f32[512]{0:T(512)S(1)} fusion(f32[1024]{0:T(1024)S(1)} %copy-done, s32[1024]{0:T(1024)S(1)} %pad_clamp_fusion), kind=kCustom, calls=%fused_computation.1 | custom fusion | bytes 6144 | tf_op jit(solution)/shard_map/jit(_take)/gather | solution.py:21
  9.5 0.7 broadcast_select_fusion.1
  10.2 1.1 copy.9
  11.3 1.3 gather_fusion
  12.7 0.1 broadcast_select_fusion
  12.8 0.7 copy.10
  13.5 0.0 all-gather.2.cloned.1.call-update
  13.6 0.0 reduce-scatter.2.cloned.1.call-start
  13.6 0.8 dynamic_slice.10
  14.4 0.8 dynamic_slice.9
  15.1 0.0 copy-start.1
  15.1 160.4 %all-gather.2.cloned.1.call-done = bf16[512,8192]{0,1:T(8,128)(2,1)} async-done(((bf16[512,64]{0,1:T(8,128)(2,1)}), bf16[512,8192]{0,1:T(8,128)(2,1)}) %all-gather.2.cloned.1.call-update) | async-done | bytes 8388624 | tf_op jit(solution)/shard_map/all_gather | solution.py:19
  175.5 9.0 %fusion = f32[512,256]{1,0:T(8,128)} fusion(bf16[512,8192]{0,1:T(8,128)(2,1)} %all-gather.2.cloned.1.call-done, bf16[8192,256]{1,0:T(8,128)(2,1)} %param.7, s32[256]{0:T(256)S(1)} %dynamic_slice.10, s32[8192]{0:T(1024)S(1)} %dynamic_slice.9), kind=kOutput, calls=%fused_computation.3 | convolution fusion | flops 2151677952 | bytes 13140992 | tf_op jit(solution)/shard_map/dot_general | solution.py:20
  184.5 0.0 reduce-scatter.2.cloned.1.call-update
  184.6 0.1 dynamic_slice.11
  184.6 20.9 %reduce-scatter.2.cloned.1.call-done = f32[128,256]{1,0:T(8,128)} async-done(((f32[512,256]{1,0:T(8,128)}), f32[128,256]{1,0:T(8,128)}) %reduce-scatter.2.cloned.1.call-update) | async-done | bytes 131088 | tf_op jit(solution)/shard_map/reduce_scatter | solution.py:23
  205.5 0.0 copy-done.1
  205.6 1.6 divide_convert_fusion
  (1 shorter events, 0.0 us)
Async XLA Ops:
  6.5 0.7 copy-start
  6.5 169.0 %all-gather.2.cloned.1.call-start = ((), (), s32[]{:S(2)}) async-start(), calls=%async_computation.1 | async-start | bytes 8454144 | tf_op jit(solution)/shard_map/all_gather | solution.py:19
  13.6 192.0 %reduce-scatter.2.cloned.1.call-start = ((), (), s32[]{:S(2)}) async-start(), calls=%async_computation.2 | async-start | bytes 655360 | tf_op jit(solution)/shard_map/reduce_scatter | solution.py:23
  15.1 190.4 %copy-start.1 = (f32[256]{0:T(256)S(1)}, f32[256]{0:T(256)}, u32[]{:S(2)}) copy-start(f32[256]{0:T(256)} %param.10) | copy-start | bytes 3076
Sparse Core Ops, SparseCore 0:
  13.7 161.8 all-gather.1
  184.7 20.8 reduce-scatter.1
where the time goes:
time: 215 us; the launch traced here: 214 us
  waiting for transfers between devices  181 us (84%)
  between operations  13.4 us (6%)
  matrix products  9 us (4%)
  local copies, waits for them, and re-layouts  7.03 us (3%)
  other arithmetic  3.16 us (1%)
    all_gather x1, waiting for transfers between devices, body(): gathered = lax.all_gather(chosen, 'blk', axis=1, tiled=True)  160 us
    reduce_scatter x1, waiting for transfers between devices, body(): owned = lax.psum_scatter(ladder, 'grp', scatter_dimension=0, tiled=True)  20.9 us
    dot_general x1, matrix products, body(): ladder = jnp.dot(gathered, masked, preferred_element_type=jnp.float32)  9 us
  transfers between devices with their start and end apart: 2, of which 2 were waited for; matrix products, arithmetic and copies ran while one was open for 1% of the time, Pallas kernels for 0%

commit v1 on v0

v1 whole, which is shorter than its diff:
```python
import functools

import jax
import jax.numpy as jnp
from jax import lax
from jax.experimental import pallas as pl
from jax.experimental.pallas import tpu as pltpu
from jax.sharding import PartitionSpec as P

H, Z, X, C = 2, 8, 4, 2
SHARD = 64
OCC = 512
QUARTER = 8192
COLS = 256
GRP = 4
OWN = OCC // GRP
VMEM_LIMIT = 50 * 1024 * 1024


def index(h, z, x, c):
    return ((h % H * Z + z % Z) * X + x % X) * C + c


def devices():
    return [(h, z, x, c) for h in range(H) for z in range(Z) for x in range(X) for c in range(C)]


def groups():
    first = [[index(h, z, x, 0) for h in range(H) for x in range(X)] for z in range(Z)]
    second = [[index(h, z, x, 1) for z in range(Z)] for h in range(H) for x in range(X)]
    return first + second


def ring(step, cores=(0, 1)):
    pairs = []
    for h, z, x, c in devices():
        if c in cores:
            target = index(h, z + step, x, 0) if c == 0 else index(h, z, x + step, 1)
            pairs.append((index(h, z, x, c), target))
    return pairs


def across_h():
    return [(index(h, z, x, 1), index(h + 1, z, x, 1)) for h, z, x, c in devices() if c == 1]


def across_core():
    return [(index(h, z, x, c), index(h, z, x, 1 - c)) for h, z, x, c in devices()]


def select_kernel(amp_ref, subset_ref, out_ref):
    rows = amp_ref.shape[1]
    hot = (lax.broadcasted_iota(jnp.int32, (rows, OCC), 0) == subset_ref[...]).astype(jnp.bfloat16)
    chosen = jnp.dot(amp_ref[...], hot, preferred_element_type=jnp.float32).astype(jnp.bfloat16)
    for copy in range(8):
        out_ref[pl.ds(copy * SHARD, SHARD), :] = chosen


def select(amplitudes, subset):
    return pl.pallas_call(
        select_kernel,
        out_shape=jax.ShapeDtypeStruct((8 * SHARD, OCC), jnp.bfloat16),
        in_specs=[pl.BlockSpec(memory_space=pltpu.VMEM)] * 2,
        out_specs=pl.BlockSpec(memory_space=pltpu.VMEM),
        compiler_params=pltpu.CompilerParams(vmem_limit_bytes=VMEM_LIMIT),
        name="select",
    )(amplitudes, subset)


def ladder_kernel(place_ref, *refs):
    pieces, (plus4_ref, minus4_ref, across_ref, ints_ref, got_ref, low_ref, high_ref, out_ref, last_ref, acc_ref) = refs[:7], refs[7:]
    core = place_ref[64]
    start = place_ref[65]

    @pl.when(core == 0)
    def _():
        last_ref[pl.ds(0, 256), :] = plus4_ref[...]
        last_ref[pl.ds(256, 256), :] = minus4_ref[...]

    @pl.when(core == 1)
    def _():
        last_ref[...] = across_ref[...]

    low, high = low_ref[...], high_ref[...]
    for number, piece_ref in enumerate(pieces + (last_ref,)):
        parts = []
        for chunk in range(8):
            shard = place_ref[number * 8 + chunk]
            here = pl.multiple_of((2 * shard + core) * SHARD, SHARD)
            there = pl.multiple_of(shard * SHARD, SHARD)
            values = jnp.concatenate([ints_ref[pl.ds(here, SHARD), :], got_ref[pl.ds(there, SHARD), :]], axis=1)
            row = start + here + lax.broadcasted_iota(jnp.int32, values.shape, 0)
            keep = (row >= low) & (row < high)
            parts.append(jnp.where(keep, values, jnp.zeros_like(values)))
        masked = jnp.concatenate(parts, axis=0)
        term = lax.dot_general(masked, piece_ref[...], (((0,), (0,)), ((), ())), preferred_element_type=jnp.float32)
        if number == 0:
            acc_ref[...] = term
        else:
            acc_ref[...] += term
    for half in range(2):
        for owner in range(GRP):
            out_ref[half, owner] = acc_ref[pl.ds(half * COLS, COLS), pl.ds(owner * OWN, OWN)]


def ladder(place, pieces, plus4, minus4, across, ints, got, low, high):
    vmem = pl.BlockSpec(memory_space=pltpu.VMEM)
    return pl.pallas_call(
        ladder_kernel,
        out_shape=jax.ShapeDtypeStruct((2, GRP, COLS, OWN), jnp.float32),
        in_specs=[pl.BlockSpec(memory_space=pltpu.SMEM)] + [vmem] * 14,
        out_specs=vmem,
        scratch_shapes=[pltpu.VMEM((512, OCC), jnp.bfloat16), pltpu.VMEM((2 * COLS, OCC), jnp.float32)],
        compiler_params=pltpu.CompilerParams(vmem_limit_bytes=VMEM_LIMIT),
        cost_estimate=pl.CostEstimate(flops=2 * 512 * 512 * 4096, bytes_accessed=11 << 20, transcendentals=0),
        name="ladder",
    )(place, *pieces, plus4, minus4, across, ints, got, low, high)


def deal_kernel(me_ref, mine_ref, other_ref, *out_refs):
    me = me_ref[0]
    for step, out_ref in enumerate(out_refs):
        owner = lax.rem(me + step, GRP)
        out_ref[...] = mine_ref[0, owner] + other_ref[owner]


def deal(me, mine, other):
    vmem = pl.BlockSpec(memory_space=pltpu.VMEM)
    return pl.pallas_call(
        deal_kernel,
        out_shape=[jax.ShapeDtypeStruct((COLS, OWN), jnp.float32)] * GRP,
        in_specs=[pl.BlockSpec(memory_space=pltpu.SMEM), vmem, vmem],
        out_specs=[vmem] * GRP,
        compiler_params=pltpu.CompilerParams(vmem_limit_bytes=VMEM_LIMIT),
        name="deal",
    )(me, mine, other)


def close_kernel(a_ref, b_ref, c_ref, d_ref, gap_ref, vir_ref, out_ref):
    total = a_ref[...] + b_ref[...] + c_ref[...] + d_ref[...]
    out_ref[...] = (total.T / (gap_ref[...] + vir_ref[...])).astype(jnp.bfloat16)


def close(terms, gaps, vir):
    vmem = pl.BlockSpec(memory_space=pltpu.VMEM)
    return pl.pallas_call(
        close_kernel,
        out_shape=jax.ShapeDtypeStruct((OWN, COLS), jnp.bfloat16),
        in_specs=[vmem] * 6,
        out_specs=vmem,
        compiler_params=pltpu.CompilerParams(vmem_limit_bytes=VMEM_LIMIT),
        name="close",
    )(*terms, gaps, vir)


def body(amplitudes, ladder_ints, pair_irrep, occ_gap, vir_energy, pair_subset):
    me = lax.axis_index("grp").astype(jnp.int32)
    blk = lax.axis_index("blk").astype(jnp.int32)
    c = blk % 2
    x = blk // 2 % X
    z = blk // 8 % Z
    h = blk // 64
    permute = functools.partial(lax.ppermute, axis_name="blk")

    amp = jnp.transpose(amplitudes[:, 0, :])
    copies = select(amp, pair_subset[None, :])
    own = lax.all_to_all(copies, "blk", 0, 0, axis_index_groups=groups(), tiled=True)

    pairs = ladder_ints.reshape(64, 2, SHARD, COLS)
    away = lax.dynamic_index_in_dim(pairs, 1 - c, axis=1, keepdims=False).reshape(64 * SHARD, COLS)
    got = permute(away, perm=across_core())

    plus, minus = ring(1), ring(-1)
    across = permute(own, perm=across_h())
    p1 = permute(own, perm=plus)
    m1 = permute(own, perm=minus)
    p2 = permute(p1, perm=plus)
    m2 = permute(jnp.where(c == 0, m1, across), perm=minus)
    p3 = permute(jnp.where(c == 0, p2, across), perm=plus)
    m3 = permute(m2, perm=minus)
    p4 = permute(p3[:256], perm=ring(1, (0,)))
    m4 = permute(m3[256:], perm=ring(-1, (0,)))

    t = jnp.arange(8, dtype=jnp.int32)
    z_from = [z, z - 1, z + 1, z - 2, z + 2, z - 3, z + 3, z + 4]
    zeros = [(t // 4 * Z + zz % Z) * X + t % 4 for zz in z_from]
    hx_from = [(h, x), (h, x - 1), (h, x + 1), (h, x - 2), (h + 1, x + 1), (h + 1, x - 1), (h + 1, x + 2), (h + 1, x)]
    ones = [(hh % H * Z + t) * X + xx % X for hh, xx in hx_from]
    shards = jnp.where(c == 0, jnp.concatenate(zeros), jnp.concatenate(ones))
    place = jnp.concatenate([shards, c[None], (me * QUARTER)[None]]).astype(jnp.int32)

    counts = jnp.sum((pair_irrep[None, :] < jnp.arange(9, dtype=jnp.int32)[:, None]).astype(jnp.int32), axis=1)
    labels = jnp.concatenate([
        lax.dynamic_slice_in_dim(pair_irrep, blk * COLS, COLS, 0),
        lax.dynamic_slice_in_dim(pair_irrep, (blk + 1 - 2 * c) * COLS, COLS, 0),
    ])
    is_label = labels[None, :] == jnp.arange(8, dtype=jnp.int32)[:, None]
    low = jnp.sum(jnp.where(is_label, counts[:8, None], 0), axis=0)[None, :]
    high = jnp.sum(jnp.where(is_label, counts[1:, None], 0), axis=0)[None, :]

    parts = ladder(place, (own, p1, m1, p2, m2, p3, m3), p4, m4, across, ladder_ints, got, low, high)
    other = permute(parts[1], perm=across_core())
    dealt = deal(me[None], parts, other)
    terms = [dealt[0]] + [
        lax.ppermute(dealt[step], "grp", [(i, (i + step) % GRP) for i in range(GRP)]) for step in range(1, GRP)
    ]
    own_subset = lax.dynamic_slice_in_dim(pair_subset, me * OWN, OWN, 0)
    gaps = jnp.take(occ_gap, own_subset)
    return close(terms, gaps[:, None], vir_energy[None, :])


def solution(mesh):
    return jax.shard_map(
        body,
        mesh=mesh,
        in_specs=(P(None, "grp", "blk"), P("grp", "blk"), P(), P(), P("blk"), P()),
        out_specs=P("grp", "blk"),
        check_vma=False,
    )
```

time: 215 us -> 118 us (0.55)
  waiting for transfers between devices: 181 us -> 14.8 us
  starting transfers between devices: 0.04 us -> 60.9 us
  blocking collectives: 0 us -> 22.8 us
  between operations: 13.4 us -> 0.65 us
  matrix products: 9 us -> 0 us
  Pallas kernels: 0 us -> 7.78 us
    all_gather x1 -> x0, waiting for transfers between devices: 160 us -> none  [body(): gathered = lax.all_gather(chosen, 'blk', axis=1, tiled=True)]
    ppermute x0 -> x14, starting transfers between devices: none -> 60.9 us  [the longest x1 16.8 us: body(): other = permute(parts[1], perm=across_core())]
    all_to_all x0 -> x1, blocking collectives: none -> 22.8 us  [body(): lax.all_to_all(copies, 'blk', 0, 0, axis_index_groups=groups(), tiled=True)]
    reduce_scatter x1 -> x0, waiting for transfers between devices: 20.9 us -> none  [body(): owned = lax.psum_scatter(ladder, 'grp', scatter_dimension=0, tiled=True)]
    ppermute x0 -> x14, waiting for transfers between devices: none -> 14.8 us  [the longest x1 4.76 us: body(): m3 = permute(m2, perm=minus)]
    dot_general x1 -> x0, matrix products: 9 us -> none  [body(): ladder = jnp.dot(gathered, masked, preferred_element_type=jnp.float32)]
    pallas_call x0 -> x4, Pallas kernels: none -> 7.78 us  [the longest x1 6.61 us: ladder(): pl.pallas_call(ladder_kernel, out_shape=jax.ShapeDtypeStruct((2, GRP, COL...]
    gather x2 -> x1, local copies, waits for them, and re-layouts: 3.63 us -> 0.97 us  [body(): gaps = jnp.take(occ_gap, own_subset)]
  transfers between devices with their start and end apart: 2 -> 14, of which waited for: 2 -> 5; matrix products, arithmetic and copies ran while one was open for 1% -> 6% of each run, Pallas kernels for 0% -> 0%
where the time goes in v1:
time: 118 us; the launch traced here: 116 us
  starting transfers between devices  60.9 us (52%)
  blocking collectives  22.8 us (19%)
  waiting for transfers between devices  14.8 us (13%)
  Pallas kernels  7.78 us (7%)
  local copies, waits for them, and re-layouts  7.39 us (6%)
  other arithmetic  1.95 us (2%)
    all_to_all x1, blocking collectives, body(): lax.all_to_all(copies, 'blk', 0, 0, axis_index_groups=groups(), tiled=True)  22.8 us
    ppermute x1, starting transfers between devices, body(): other = permute(parts[1], perm=across_core())  16.8 us
    ppermute x3, starting transfers between devices, body(): lax.ppermute(dealt[step], 'grp', [(i, (i + step) % GRP) for i in range(GR...  11.4 us
    ppermute x1, starting transfers between devices, body(): across = permute(own, perm=across_h())  7.44 us
    ppermute x1, starting transfers between devices, body(): got = permute(away, perm=across_core())  6.88 us
    pallas_call x1, Pallas kernels, ladder(): pl.pallas_call(ladder_kernel, out_shape=jax.ShapeDtypeStruct((2, GRP, COL...  6.61 us
    ppermute x1, waiting for transfers between devices, body(): m3 = permute(m2, perm=minus)  4.76 us
    ppermute x1, waiting for transfers between devices, body(): m2 = permute(jnp.where(c == 0, m1, across), perm=minus)  4.43 us
  transfers between devices with their start and end apart: 14, of which 5 were waited for; matrix products, arithmetic and copies ran while one was open for 6% of the time, Pallas kernels for 0%

profile of v1, /device:TPU:1, one launch (start us, length us, event | category | flops | bytes accessed | tf_op | source)
XLA Modules:
  0.0 116.3 jit_solution(10242626196035597902)
XLA Ops:
  0.0 0.0 copy-start
  0.0 0.0 copy-start.2
  0.0 0.9 copy-done.2
  0.9 0.0 copy-start.3
  0.9 0.7 copy-done.3
  1.6 0.3 select.55
  1.9 22.8 %all_to_all.11 = bf16[8,64,512]{2,1,0:T(8,128)(2,1)S(1)} all-to-all(bf16[8,64,512]{2,1,0:T(8,128)(2,1)S(1)} %bitcast.24), channel_id=1, replica_groups={{0,8,16,24,256,264,272,280},{32,40,48,56,288,296,304,312},{64,72,80,88,..., dimensions={0} | all-to-all | bytes 1048576 | tf_op jit(solution)/shard_map/all_to_all | solution.py:167
  24.7 3.1 %collective-permute-start = (bf16[512,512]{1,0:T(8,128)(2,1)S(1)}, bf16[512,512]{1,0:T(8,128)(2,1)S(1)}, u32[]{:S(2)}, u32[]{:S(2)}) collective-permute-start(bf16[512,512]{1,0:T(8,128)(2,1)S(1)} %bitcast.20), channel_id=1, source_target_pairs={{0,32},{4,12},{8,40},{12,20},{16,48},{20,28},{24,56},{28,4},{32,64... | collective-permute-start | bytes 1572872 | tf_op jit(solution)/shard_map/ppermute | solution.py:175
  27.9 3.4 %collective-permute-start.1 = (bf16[512,512]{1,0:T(8,128)(2,1)S(1)}, bf16[512,512]{1,0:T(8,128)(2,1)S(1)}, u32[]{:S(2)}, u32[]{:S(2)}) collective-permute-start(bf16[512,512]{1,0:T(8,128)(2,1)S(1)} %bitcast.21), channel_id=1, source_target_pairs={{0,224},{4,28},{8,232},{12,4},{16,240},{20,12},{24,248},{28,20},{3... | collective-permute-start | bytes 1572872 | tf_op jit(solution)/shard_map/ppermute | solution.py:176
  31.3 7.4 %collective-permute-start.3 = (bf16[512,512]{1,0:T(8,128)(2,1)S(1)}, bf16[512,512]{1,0:T(8,128)(2,1)S(1)}, u32[]{:S(2)}, u32[]{:S(2)}) collective-permute-start(bf16[512,512]{1,0:T(8,128)(2,1)S(1)} %bitcast.22), channel_id=1, source_target_pairs={{4,260},{12,268},{20,276},{28,284},{36,292},{44,300},{52,308},{60,... | collective-permute-start | bytes 1572872 | tf_op jit(solution)/shard_map/ppermute | solution.py:174
  38.7 0.0 collective-permute-done.refs_1_
  38.7 1.9 %collective-permute-start.2 = (bf16[512,512]{1,0:T(8,128)(2,1)S(1)}, bf16[512,512]{1,0:T(8,128)(2,1)S(1)}, u32[]{:S(2)}, u32[]{:S(2)}) collective-permute-start(bf16[512,512]{1,0:T(8,128)(2,1)S(1)} %collective-permute-done.refs_1_), channel_id=1, source_target_pairs={{0,32},{4,12},{8,40},{12,20},{16,48},{20,28},{24,56},{28,4},{32,64... | collective-permute-start | bytes 1572872 | tf_op jit(solution)/shard_map/ppermute | solution.py:177
  40.7 3.2 %constant_dynamic-slice_fusion = bf16[64,1,64,256]{3,2,1,0:T(8,128)(2,1)} fusion(bf16[64,2,64,256]{3,2,1,0:T(8,128)(2,1)} %bitcast.30, s32[]{:T(128)S(6)} %select_n.244), kind=kLoop, calls=%fused_computation.40 | loop fusion | bytes 4194308 | tf_op jit(solution)/shard_map/jit(dynamic_index_in_dim)/dynamic_slice | solution.py:170
  43.8 0.0 copy-start.8
  43.8 6.9 %collective-permute-start.9 = (bf16[4096,256]{1,0:T(8,128)(2,1)}, bf16[4096,256]{1,0:T(8,128)(2,1)}, u32[]{:S(2)}, u32[]{:S(2)}) collective-permute-start(bf16[4096,256]{1,0:T(8,128)(2,1)} %bitcast.9), channel_id=1, source_target_pairs={{0,4},{4,0},{8,12},{12,8},{16,20},{20,16},{24,28},{28,24},{32,36},... | collective-permute-start | bytes 6291464 | tf_op jit(solution)/shard_map/ppermute | solution.py:171
  51.0 0.0 collective-permute-done.1.refs_2_
  51.0 0.0 collective-permute-done.3.refs_9_
  51.0 0.0 copy-start.6
  51.0 0.0 collective-permute-done.2.refs_3_
  51.0 1.2 %broadcast_select_fusion = (bf16[512,512]{1,0:T(8,128)(2,1)}, bf16[512,512]{1,0:T(8,128)(2,1)}) fusion(bf16[512,512]{1,0:T(8,128)(2,1)S(1)} %collective-permute-done.2.refs_3_, bf16[512,512]{1,0:T(8,128)(2,1)S(1)} %collective-permute-done.3.refs_9_, pred[]{:T(512)S(6)} %eq.55, bf16[512,512]{1,0:T(8,128)(2,1)S(1)} %collective-permute-done.1.refs_2_), kind=kLoop, calls=%fused_computation.4 | loop fusion | flops 524288 | bytes 2621441 | tf_op jit(solution)/shard_map/jit(_where)/select_n | solution.py:179
  52.2 2.5 %collective-permute-start.4 = (bf16[512,512]{1,0:T(8,128)(2,1)}, bf16[512,512]{1,0:T(8,128)(2,1)S(1)}, u32[]{:S(2)}, u32[]{:S(2)}) collective-permute-start(bf16[512,512]{1,0:T(8,128)(2,1)} %get-tuple-element.16), channel_id=1, source_target_pairs={{0,224},{4,28},{8,232},{12,4},{16,240},{20,12},{24,248},{28,20},{3... | collective-permute-start | bytes 1572872 | tf_op jit(solution)/shard_map/ppermute | solution.py:178
  54.8 0.1 concatenate.13
  54.9 0.1 concatenate.12
  55.0 0.0 copy-done.8
  55.0 0.4 convert_reduce_fusion
  55.4 2.8 %collective-permute-start.5 = (bf16[512,512]{1,0:T(8,128)(2,1)}, bf16[512,512]{1,0:T(8,128)(2,1)S(1)}, u32[]{:S(2)}, u32[]{:S(2)}) collective-permute-start(bf16[512,512]{1,0:T(8,128)(2,1)} %get-tuple-element.15), channel_id=1, source_target_pairs={{0,32},{4,12},{8,40},{12,20},{16,48},{20,28},{24,56},{28,4},{32,64... | collective-permute-start | bytes 1572872 | tf_op jit(solution)/shard_map/ppermute | solution.py:179
  58.2 4.4 %collective-permute-done.4.refs_4_ = bf16[512,512]{1,0:T(8,128)(2,1)S(1)} collective-permute-done((bf16[512,512]{1,0:T(8,128)(2,1)}, bf16[512,512]{1,0:T(8,128)(2,1)S(1)}, u32[]{:S(2)}, u32[]{:S(2)}) %collective-permute-start.4) | collective-permute-done | bytes 524320 | tf_op jit(solution)/shard_map/ppermute | solution.py:178
  62.6 3.4 %collective-permute-start.6 = (bf16[512,512]{1,0:T(8,128)(2,1)S(1)}, bf16[512,512]{1,0:T(8,128)(2,1)S(1)}, u32[]{:S(2)}, u32[]{:S(2)}) collective-permute-start(bf16[512,512]{1,0:T(8,128)(2,1)S(1)} %collective-permute-done.4.refs_4_), channel_id=1, source_target_pairs={{0,224},{4,28},{8,232},{12,4},{16,240},{20,12},{24,248},{28,20},{3... | collective-permute-start | bytes 1572872 | tf_op jit(solution)/shard_map/ppermute | solution.py:180
  66.0 0.1 fusion.2
  66.1 0.1 fusion.3
  66.2 0.9 collective-permute-done.5.refs_5_
  67.0 0.7 collective-permute-start.7
  67.7 4.8 %collective-permute-done.6.refs_6_ = bf16[512,512]{1,0:T(8,128)(2,1)S(1)} collective-permute-done((bf16[512,512]{1,0:T(8,128)(2,1)S(1)}, bf16[512,512]{1,0:T(8,128)(2,1)S(1)}, u32[]{:S(2)}, u32[]{:S(2)}) %collective-permute-start.6) | collective-permute-done | bytes 524320 | tf_op jit(solution)/shard_map/ppermute | solution.py:180
  72.5 0.0 copy-start.7
  72.5 0.7 collective-permute-start.8
  73.2 0.1 pad_add_fusion.1.place_ref
  73.3 0.1 select_reduce_fusion
  73.4 0.0 collective-permute-done.9.refs_11_
  73.4 0.0 collective-permute-done.7.refs_7_
  73.4 0.0 collective-permute-done.8.refs_8_
  73.4 0.0 copy-done.6
  73.4 0.0 copy-done.7
  73.4 0.0 copy-start.4
  73.4 6.6 %ladder.1.mine_ref = f32[2,4,256,128]{3,2,1,0:T(8,128)} custom-call(s32[66]{0:T(128)S(1)} %pad_add_fusion.1.place_ref, bf16[512,512]{1,0:T(8,128)(2,1)S(1)} %bitcast.23, bf16[512,512]{1,0:T(8,128)(2,1)S(1)} %collective-permute-done.refs_1_, bf16[512,512]{1,0:T(8,128)(2,1)S(1)} %collective-permute-done.1.refs_2_, ...), custom_call_target="tpu_custom_call" | custom-call | flops 2147483648 | bytes 11534336 | tf_op jit(solution)/shard_map/ladder/pallas_call | solution.py:108
  80.1 0.0 copy-start.1
  80.1 1.2 %slice_bitcast_fusion = f32[4,256,128]{2,1,0:T(8,128)S(1)} fusion(f32[2,4,256,128]{3,2,1,0:T(8,128)} %ladder.1.mine_ref), kind=kLoop, calls=%fused_computation.3 | loop fusion | bytes 1048576 | tf_op jit(solution)/shard_map/squeeze | solution.py:202
  81.2 16.8 %collective-permute-start.10 = (f32[4,256,128]{2,1,0:T(8,128)S(1)}, f32[4,256,128]{2,1,0:T(8,128)S(1)}, u32[]{:S(2)}, u32[]{:S(2)}) collective-permute-start(f32[4,256,128]{2,1,0:T(8,128)S(1)} %slice_bitcast_fusion), channel_id=1, source_target_pairs={{0,4},{4,0},{8,12},{12,8},{16,20},{20,16},{24,28},{28,24},{32,36},... | collective-permute-start | bytes 1572872 | tf_op jit(solution)/shard_map/ppermute | solution.py:202
  98.0 0.0 copy-done.4
  98.0 0.1 compare_select_fusion
  98.1 0.0 copy-done
  98.1 1.0 gather_fusion
  99.1 0.4 collective-permute-done.10.other_ref
  99.5 0.0 copy-done.1
  99.5 0.1 deal.1
  99.6 5.0 %collective-permute-start.11 = (f32[256,128]{1,0:T(8,128)S(1)}, f32[256,128]{1,0:T(8,128)S(1)}, u32[]{:S(2)}, u32[]{:S(2)}) collective-permute-start(f32[256,128]{1,0:T(8,128)S(1)} %get-tuple-element.10), channel_id=1, source_target_pairs={{0,1},{1,2},{2,3},{3,0},{4,5},{5,6},{6,7},{7,4},{8,9},{9,10},{10,1... | collective-permute-start | bytes 393224 | tf_op jit(solution)/shard_map/ppermute | solution.py:205
  104.6 2.1 %collective-permute-start.12 = (f32[256,128]{1,0:T(8,128)S(1)}, f32[256,128]{1,0:T(8,128)S(1)}, u32[]{:S(2)}, u32[]{:S(2)}) collective-permute-start(f32[256,128]{1,0:T(8,128)S(1)} %get-tuple-element.11), channel_id=1, source_target_pairs={{0,2},{1,3},{2,0},{3,1},{4,6},{5,7},{6,4},{7,5},{8,10},{9,11},{10,... | collective-permute-start | bytes 393224 | tf_op jit(solution)/shard_map/ppermute | solution.py:205
  106.7 4.3 %collective-permute-start.13 = (f32[256,128]{1,0:T(8,128)S(1)}, f32[256,128]{1,0:T(8,128)S(1)}, u32[]{:S(2)}, u32[]{:S(2)}) collective-permute-start(f32[256,128]{1,0:T(8,128)S(1)} %get-tuple-element.12), channel_id=1, source_target_pairs={{0,3},{1,0},{2,1},{3,2},{4,7},{5,4},{6,5},{7,6},{8,11},{9,8},{10,9... | collective-permute-start | bytes 393224 | tf_op jit(solution)/shard_map/ppermute | solution.py:205
  111.0 0.1 fusion.1
  111.1 0.1 copy.12.gap_ref
  111.2 0.0 collective-permute-done.11.b_ref
  111.2 4.3 %collective-permute-done.12.c_ref = f32[256,128]{1,0:T(8,128)S(1)} collective-permute-done((f32[256,128]{1,0:T(8,128)S(1)}, f32[256,128]{1,0:T(8,128)S(1)}, u32[]{:S(2)}, u32[]{:S(2)}) %collective-permute-start.12) | collective-permute-done | bytes 131104 | tf_op jit(solution)/shard_map/ppermute | solution.py:205
  115.5 0.0 collective-permute-done.13.d_ref
  115.5 0.0 copy-done.5
  115.5 0.8 close.1
  (14 shorter events, 0.1 us)
Async XLA Ops:
  0.0 98.1 %copy-start = (f32[1024]{0:T(1024)S(1)}, f32[1024]{0:T(1024)}, u32[]{:S(2)}) copy-start(f32[1024]{0:T(1024)} %param.9) | copy-start | bytes 12292
  0.0 0.9 copy-start.2
  0.9 0.7 copy-start.3
  24.7 14.0 %collective-permute-start = (bf16[512,512]{1,0:T(8,128)(2,1)S(1)}, bf16[512,512]{1,0:T(8,128)(2,1)S(1)}, u32[]{:S(2)}, u32[]{:S(2)}) collective-permute-start(bf16[512,512]{1,0:T(8,128)(2,1)S(1)} %bitcast.20), channel_id=1, source_target_pairs={{0,32},{4,12},{8,40},{12,20},{16,48},{20,28},{24,56},{28,4},{32,64... | collective-permute-start | bytes 1572872 | tf_op jit(solution)/shard_map/ppermute | solution.py:175
  27.9 23.1 %collective-permute-start.1 = (bf16[512,512]{1,0:T(8,128)(2,1)S(1)}, bf16[512,512]{1,0:T(8,128)(2,1)S(1)}, u32[]{:S(2)}, u32[]{:S(2)}) collective-permute-start(bf16[512,512]{1,0:T(8,128)(2,1)S(1)} %bitcast.21), channel_id=1, source_target_pairs={{0,224},{4,28},{8,232},{12,4},{16,240},{20,12},{24,248},{28,20},{3... | collective-permute-start | bytes 1572872 | tf_op jit(solution)/shard_map/ppermute | solution.py:176
  31.3 19.7 %collective-permute-start.3 = (bf16[512,512]{1,0:T(8,128)(2,1)S(1)}, bf16[512,512]{1,0:T(8,128)(2,1)S(1)}, u32[]{:S(2)}, u32[]{:S(2)}) collective-permute-start(bf16[512,512]{1,0:T(8,128)(2,1)S(1)} %bitcast.22), channel_id=1, source_target_pairs={{4,260},{12,268},{20,276},{28,284},{36,292},{44,300},{52,308},{60,... | collective-permute-start | bytes 1572872 | tf_op jit(solution)/shard_map/ppermute | solution.py:174
  38.7 12.3 %collective-permute-start.2 = (bf16[512,512]{1,0:T(8,128)(2,1)S(1)}, bf16[512,512]{1,0:T(8,128)(2,1)S(1)}, u32[]{:S(2)}, u32[]{:S(2)}) collective-permute-start(bf16[512,512]{1,0:T(8,128)(2,1)S(1)} %collective-permute-done.refs_1_), channel_id=1, source_target_pairs={{0,32},{4,12},{8,40},{12,20},{16,48},{20,28},{24,56},{28,4},{32,64... | collective-permute-start | bytes 1572872 | tf_op jit(solution)/shard_map/ppermute | solution.py:177
  43.8 11.2 %copy-start.8 = (s32[32768]{0:T(1024)S(1)}, s32[32768]{0:T(1024)}, u32[]{:S(2)}) copy-start(s32[32768]{0:T(1024)} %param.8) | copy-start | bytes 393220
  43.8 29.6 %collective-permute-start.9 = (bf16[4096,256]{1,0:T(8,128)(2,1)}, bf16[4096,256]{1,0:T(8,128)(2,1)}, u32[]{:S(2)}, u32[]{:S(2)}) collective-permute-start(bf16[4096,256]{1,0:T(8,128)(2,1)} %bitcast.9), channel_id=1, source_target_pairs={{0,4},{4,0},{8,12},{12,8},{16,20},{20,16},{24,28},{28,24},{32,36},... | collective-permute-start | bytes 6291464 | tf_op jit(solution)/shard_map/ppermute | solution.py:171
  51.0 22.4 %copy-start.6 = (bf16[512,512]{1,0:T(8,128)(2,1)}, bf16[512,512]{1,0:T(8,128)(2,1)S(1)}, u32[]{:S(2)}) copy-start(bf16[512,512]{1,0:T(8,128)(2,1)S(1)} %collective-permute-done.3.refs_9_) | copy-start | bytes 1572868
  52.2 10.4 %collective-permute-start.4 = (bf16[512,512]{1,0:T(8,128)(2,1)}, bf16[512,512]{1,0:T(8,128)(2,1)S(1)}, u32[]{:S(2)}, u32[]{:S(2)}) collective-permute-start(bf16[512,512]{1,0:T(8,128)(2,1)} %get-tuple-element.16), channel_id=1, source_target_pairs={{0,224},{4,28},{8,232},{12,4},{16,240},{20,12},{24,248},{28,20},{3... | collective-permute-start | bytes 1572872 | tf_op jit(solution)/shard_map/ppermute | solution.py:178
  55.4 11.6 %collective-permute-start.5 = (bf16[512,512]{1,0:T(8,128)(2,1)}, bf16[512,512]{1,0:T(8,128)(2,1)S(1)}, u32[]{:S(2)}, u32[]{:S(2)}) collective-permute-start(bf16[512,512]{1,0:T(8,128)(2,1)} %get-tuple-element.15), channel_id=1, source_target_pairs={{0,32},{4,12},{8,40},{12,20},{16,48},{20,28},{24,56},{28,4},{32,64... | collective-permute-start | bytes 1572872 | tf_op jit(solution)/shard_map/ppermute | solution.py:179
  62.6 9.9 %collective-permute-start.6 = (bf16[512,512]{1,0:T(8,128)(2,1)S(1)}, bf16[512,512]{1,0:T(8,128)(2,1)S(1)}, u32[]{:S(2)}, u32[]{:S(2)}) collective-permute-start(bf16[512,512]{1,0:T(8,128)(2,1)S(1)} %collective-permute-done.4.refs_4_), channel_id=1, source_target_pairs={{0,224},{4,28},{8,232},{12,4},{16,240},{20,12},{24,248},{28,20},{3... | collective-permute-start | bytes 1572872 | tf_op jit(solution)/shard_map/ppermute | solution.py:180
  67.0 6.3 %collective-permute-start.7 = (bf16[256,512]{1,0:T(8,128)(2,1)S(1)}, bf16[256,512]{1,0:T(8,128)(2,1)S(1)}, u32[]{:S(2)}, u32[]{:S(2)}) collective-permute-start(bf16[256,512]{1,0:T(8,128)(2,1)S(1)} %slice.22), channel_id=1, source_target_pairs={{0,32},{8,40},{16,48},{24,56},{32,64},{40,72},{48,80},{56,88},{64,... | collective-permute-start | bytes 786440 | tf_op jit(solution)/shard_map/ppermute | solution.py:181
  72.5 0.9 copy-start.7
  72.5 0.9 collective-permute-start.8
  73.4 24.6 %copy-start.4 = (s32[512]{0:T(512)S(1)}, s32[512]{0:T(512)}, u32[]{:S(2)}) copy-start(s32[512]{0:T(512)} %param.11) | copy-start | bytes 6148
  80.1 19.5 %copy-start.1 = (f32[2,4,256,128]{3,2,1,0:T(8,128)S(1)}, f32[2,4,256,128]{3,2,1,0:T(8,128)}, u32[]{:S(2)}) copy-start(f32[2,4,256,128]{3,2,1,0:T(8,128)} %ladder.1.mine_ref) | copy-start | bytes 3145732
  80.1 35.4 %copy-start.5 = (f32[256]{0:T(256)S(1)}, f32[256]{0:T(256)}, u32[]{:S(2)}) copy-start(f32[256]{0:T(256)} %param.10) | copy-start | bytes 3076
  81.2 18.3 %collective-permute-start.10 = (f32[4,256,128]{2,1,0:T(8,128)S(1)}, f32[4,256,128]{2,1,0:T(8,128)S(1)}, u32[]{:S(2)}, u32[]{:S(2)}) collective-permute-start(f32[4,256,128]{2,1,0:T(8,128)S(1)} %slice_bitcast_fusion), channel_id=1, source_target_pairs={{0,4},{4,0},{8,12},{12,8},{16,20},{20,16},{24,28},{28,24},{32,36},... | collective-permute-start | bytes 1572872 | tf_op jit(solution)/shard_map/ppermute | solution.py:202
  99.6 11.6 %collective-permute-start.11 = (f32[256,128]{1,0:T(8,128)S(1)}, f32[256,128]{1,0:T(8,128)S(1)}, u32[]{:S(2)}, u32[]{:S(2)}) collective-permute-start(f32[256,128]{1,0:T(8,128)S(1)} %get-tuple-element.10), channel_id=1, source_target_pairs={{0,1},{1,2},{2,3},{3,0},{4,5},{5,6},{6,7},{7,4},{8,9},{9,10},{10,1... | collective-permute-start | bytes 393224 | tf_op jit(solution)/shard_map/ppermute | solution.py:205
  104.6 10.9 %collective-permute-start.12 = (f32[256,128]{1,0:T(8,128)S(1)}, f32[256,128]{1,0:T(8,128)S(1)}, u32[]{:S(2)}, u32[]{:S(2)}) collective-permute-start(f32[256,128]{1,0:T(8,128)S(1)} %get-tuple-element.11), channel_id=1, source_target_pairs={{0,2},{1,3},{2,0},{3,1},{4,6},{5,7},{6,4},{7,5},{8,10},{9,11},{10,... | collective-permute-start | bytes 393224 | tf_op jit(solution)/shard_map/ppermute | solution.py:205
  106.7 8.8 %collective-permute-start.13 = (f32[256,128]{1,0:T(8,128)S(1)}, f32[256,128]{1,0:T(8,128)S(1)}, u32[]{:S(2)}, u32[]{:S(2)}) collective-permute-start(f32[256,128]{1,0:T(8,128)S(1)} %get-tuple-element.12), channel_id=1, source_target_pairs={{0,3},{1,0},{2,1},{3,2},{4,7},{5,4},{6,5},{7,6},{8,11},{9,8},{10,9... | collective-permute-start | bytes 393224 | tf_op jit(solution)/shard_map/ppermute | solution.py:205

commit v2 on v1

v2 whole, which is shorter than its diff:
```python
import functools

import jax
import jax.numpy as jnp
from jax import lax
from jax.experimental import pallas as pl
from jax.experimental.pallas import tpu as pltpu
from jax.sharding import PartitionSpec as P

H, Z, X, C = 2, 8, 4, 2
SHARD = 64
OCC = 512
QUARTER = 8192
COLS = 256
GRP = 4
OWN = OCC // GRP
VMEM_LIMIT = 16 * 1024 * 1024
STAGES = ((0, 1, 2), (3, 4), (5, 6), (7,))


def index(h, z, x, c):
    return ((h % H * Z + z % Z) * X + x % X) * C + c


def devices():
    return [(h, z, x, c) for h in range(H) for z in range(Z) for x in range(X) for c in range(C)]


def groups():
    first = [[index(h, z, x, 0) for h in range(H) for x in range(X)] for z in range(Z)]
    second = [[index(h, z, x, 1) for z in range(Z)] for h in range(H) for x in range(X)]
    return first + second


def ring(step, cores=(0, 1)):
    pairs = []
    for h, z, x, c in devices():
        if c in cores:
            target = index(h, z + step, x, 0) if c == 0 else index(h, z, x + step, 1)
            pairs.append((index(h, z, x, c), target))
    return pairs


def across_h():
    return [(index(h, z, x, 1), index(h + 1, z, x, 1)) for h, z, x, c in devices() if c == 1]


def across_core():
    return [(index(h, z, x, c), index(h, z, x, 1 - c)) for h, z, x, c in devices()]


def select_kernel(amp_ref, subset_ref, out_ref, held_ref, amp_here, subset_here, sems):
    fetch = [
        pltpu.make_async_copy(amp_ref, amp_here, sems.at[8]),
        pltpu.make_async_copy(subset_ref, subset_here, sems.at[9]),
    ]
    for copy in fetch:
        copy.start()
    for copy in fetch:
        copy.wait()
    rows = amp_here.shape[1]
    hot = (lax.broadcasted_iota(jnp.int32, (rows, OCC), 0) == subset_here[...]).astype(jnp.bfloat16)
    held_ref[...] = jnp.dot(amp_here[...], hot, preferred_element_type=jnp.float32).astype(jnp.bfloat16)
    copies = [
        pltpu.make_async_copy(held_ref, out_ref.at[pl.ds(copy * SHARD, SHARD), :], sems.at[copy]) for copy in range(8)
    ]
    for copy in copies:
        copy.start()
    for copy in copies:
        copy.wait()


def select(amplitudes, subset):
    return pl.pallas_call(
        select_kernel,
        out_shape=jax.ShapeDtypeStruct((8 * SHARD, OCC), jnp.bfloat16),
        in_specs=[pl.BlockSpec(memory_space=pltpu.HBM)] * 2,
        out_specs=pl.BlockSpec(memory_space=pltpu.HBM),
        scratch_shapes=[
            pltpu.VMEM((SHARD, OCC), jnp.bfloat16),
            pltpu.VMEM(amplitudes.shape, amplitudes.dtype),
            pltpu.VMEM(subset.shape, subset.dtype),
            pltpu.SemaphoreType.DMA((10,)),
        ],
        compiler_params=pltpu.CompilerParams(vmem_limit_bytes=VMEM_LIMIT),
        name="select",
    )(amplitudes, subset)


def pick_kernel(core_ref, first_ref, second_ref, out_ref):
    @pl.when(core_ref[0] == 0)
    def _():
        out_ref[...] = first_ref[...]

    @pl.when(core_ref[0] == 1)
    def _():
        out_ref[...] = second_ref[...]


def pick(core, first, second):
    vmem = pl.BlockSpec(memory_space=pltpu.VMEM)
    return pl.pallas_call(
        pick_kernel,
        out_shape=jax.ShapeDtypeStruct(first.shape, first.dtype),
        in_specs=[pl.BlockSpec(memory_space=pltpu.SMEM), vmem, vmem],
        out_specs=vmem,
        compiler_params=pltpu.CompilerParams(vmem_limit_bytes=VMEM_LIMIT),
        name="pick",
    )(core, first, second)


def prepare_kernel(place_ref, ints_ref, low_ref, high_ref, *out_refs):
    core = place_ref[64]
    start = place_ref[65]
    low, high = low_ref[...], high_ref[...]
    for number in range(8):
        parts = []
        for chunk in range(8):
            shard = place_ref[number * 8 + chunk]
            here = pl.multiple_of((2 * shard + core) * SHARD, SHARD)
            values = ints_ref[pl.ds(here, SHARD), :]
            row = start + here + lax.broadcasted_iota(jnp.int32, values.shape, 0)
            keep = (row >= low) & (row < high)
            parts.append(jnp.where(keep, values, jnp.zeros_like(values)))
        for stage, numbers in enumerate(STAGES):
            if number in numbers:
                out_refs[stage][number - numbers[0]] = jnp.concatenate(parts, axis=0).T


def prepare(place, ints, low, high):
    vmem = pl.BlockSpec(memory_space=pltpu.VMEM)
    return pl.pallas_call(
        prepare_kernel,
        out_shape=[jax.ShapeDtypeStruct((len(numbers), COLS, 512), jnp.bfloat16) for numbers in STAGES],
        in_specs=[pl.BlockSpec(memory_space=pltpu.SMEM)] + [vmem] * 3,
        out_specs=[vmem] * len(STAGES),
        compiler_params=pltpu.CompilerParams(vmem_limit_bytes=VMEM_LIMIT),
        cost_estimate=pl.CostEstimate(flops=0, bytes_accessed=12 << 20, transcendentals=0),
        name="prepare",
    )(place, ints, low, high)


def early_kernel(count, fresh, near_ref, far_ref, *refs):
    pieces, out_ref = refs[:count], refs[-1]
    for half, masked_ref in enumerate((near_ref, far_ref)):
        rows = pl.ds(half * COLS, COLS)
        total = None if fresh else refs[-2][rows, :]
        for at in range(count):
            term = jnp.dot(masked_ref[at], pieces[at][...], preferred_element_type=jnp.float32)
            total = term if total is None else total + term
        out_ref[rows, :] = total


def early(near, far, pieces, before=None):
    vmem = pl.BlockSpec(memory_space=pltpu.VMEM)
    inputs = (near, far, *pieces) + (() if before is None else (before,))
    return pl.pallas_call(
        functools.partial(early_kernel, len(pieces), before is None),
        out_shape=jax.ShapeDtypeStruct((2 * COLS, OCC), jnp.float32),
        in_specs=[vmem] * len(inputs),
        out_specs=vmem,
        compiler_params=pltpu.CompilerParams(vmem_limit_bytes=VMEM_LIMIT),
        cost_estimate=pl.CostEstimate(
            flops=len(pieces) * 2 * 512**3, bytes_accessed=len(pieces) << 20, transcendentals=0
        ),
        name="early",
    )(*inputs)


def tail_kernel(near_ref, far_ref, piece_ref, before_ref, mine_ref, away_ref):
    for half, (masked_ref, out_ref) in enumerate(((near_ref, mine_ref), (far_ref, away_ref))):
        total = before_ref[pl.ds(half * COLS, COLS), :]
        total += jnp.dot(masked_ref[0], piece_ref[...], preferred_element_type=jnp.float32)
        for owner in range(GRP):
            out_ref[owner] = total[:, owner * OWN : (owner + 1) * OWN]


def tail(near, far, piece, before):
    vmem = pl.BlockSpec(memory_space=pltpu.VMEM)
    return pl.pallas_call(
        tail_kernel,
        out_shape=[jax.ShapeDtypeStruct((GRP, COLS, OWN), jnp.float32)] * 2,
        in_specs=[vmem] * 4,
        out_specs=[vmem] * 2,
        compiler_params=pltpu.CompilerParams(vmem_limit_bytes=VMEM_LIMIT),
        cost_estimate=pl.CostEstimate(flops=2 * 512**3, bytes_accessed=4 << 20, transcendentals=0),
        name="tail",
    )(near, far, piece, before)


def deal_kernel(me_ref, mine_ref, other_ref, *out_refs):
    me = me_ref[0]
    for step, out_ref in enumerate(out_refs):
        owner = me ^ step
        out_ref[...] = mine_ref[owner] + other_ref[owner]


def deal(me, mine, other):
    vmem = pl.BlockSpec(memory_space=pltpu.VMEM)
    return pl.pallas_call(
        deal_kernel,
        out_shape=[jax.ShapeDtypeStruct((COLS, OWN), jnp.float32)] * GRP,
        in_specs=[pl.BlockSpec(memory_space=pltpu.SMEM), vmem, vmem],
        out_specs=[vmem] * GRP,
        compiler_params=pltpu.CompilerParams(vmem_limit_bytes=VMEM_LIMIT),
        name="deal",
    )(me, mine, other)


def close_kernel(a_ref, b_ref, c_ref, d_ref, gap_ref, vir_ref, out_ref):
    total = a_ref[...] + b_ref[...] + c_ref[...] + d_ref[...]
    out_ref[...] = (total.T / (gap_ref[...] + vir_ref[...])).astype(jnp.bfloat16)


def close(terms, gaps, vir):
    vmem = pl.BlockSpec(memory_space=pltpu.VMEM)
    return pl.pallas_call(
        close_kernel,
        out_shape=jax.ShapeDtypeStruct((OWN, COLS), jnp.bfloat16),
        in_specs=[vmem] * 6,
        out_specs=vmem,
        compiler_params=pltpu.CompilerParams(vmem_limit_bytes=VMEM_LIMIT),
        name="close",
    )(*terms, gaps, vir)


def body(amplitudes, ladder_ints, pair_irrep, occ_gap, vir_energy, pair_subset):
    me = lax.axis_index("grp").astype(jnp.int32)
    blk = lax.axis_index("blk").astype(jnp.int32)
    c = blk % 2
    x = blk // 2 % X
    z = blk // 8 % Z
    h = blk // 64
    permute = functools.partial(lax.ppermute, axis_name="blk")

    amp = jnp.transpose(amplitudes[:, 0, :])
    copies = select(amp, pair_subset[None, :])
    pair_irrep, ints, copies = lax.optimization_barrier((pair_irrep, ladder_ints, copies))
    got = permute(ints, perm=across_core())
    t = jnp.arange(8, dtype=jnp.int32)
    z_from = [z, z - 1, z + 1, z - 2, z + 2, z - 3, z + 3, z + 4]
    zeros = [(t // 4 * Z + zz % Z) * X + t % 4 for zz in z_from]
    hx_from = [(h, x), (h, x - 1), (h, x + 1), (h, x - 2), (h + 1, x), (h + 1, x - 1), (h + 1, x + 1), (h + 1, x + 2)]
    ones = [(hh % H * Z + t) * X + xx % X for hh, xx in hx_from]
    shards = jnp.where(c == 0, jnp.concatenate(zeros), jnp.concatenate(ones))
    place = jnp.concatenate([shards, c[None], (me * QUARTER)[None]]).astype(jnp.int32)

    counts = jnp.sum((pair_irrep[None, :] < jnp.arange(9, dtype=jnp.int32)[:, None]).astype(jnp.int32), axis=1)
    labels = jnp.concatenate([
        lax.dynamic_slice_in_dim(pair_irrep, blk * COLS, COLS, 0),
        lax.dynamic_slice_in_dim(pair_irrep, (blk + 1 - 2 * c) * COLS, COLS, 0),
    ])
    is_label = labels[None, :] == jnp.arange(8, dtype=jnp.int32)[:, None]
    low = jnp.sum(jnp.where(is_label, counts[:8, None], 0), axis=0)[None, :]
    high = jnp.sum(jnp.where(is_label, counts[1:, None], 0), axis=0)[None, :]

    own = lax.all_to_all(copies, "blk", 0, 0, axis_index_groups=groups(), tiled=True)
    near = prepare(place, ladder_ints, low[:, :COLS], high[:, :COLS])
    own, near = lax.optimization_barrier((own, near))
    plus, minus = ring(1), ring(-1)
    p1 = permute(own, perm=plus)
    m1 = permute(own, perm=minus)
    across = permute(own, perm=across_h())
    far = prepare(place, got, low[:, COLS:], high[:, COLS:])
    p2 = permute(p1, perm=plus)
    m2 = permute(m1, perm=ring(-1, (0,)))
    so_far = early(near[0], far[0], (own, p1, m1))
    p3_from = pick(c[None], p2, across)
    m3_from = pick(c[None], m2, across)
    p3 = permute(p3_from, perm=plus)
    p3, so_far = lax.optimization_barrier((p3, so_far))
    m3 = permute(m3_from, perm=minus)
    so_far = early(near[1], far[1], (p2, m3_from), so_far)
    p4 = permute(p3, perm=plus)
    so_far = early(near[2], far[2], (p3, m3), so_far)
    own_subset = lax.dynamic_slice_in_dim(pair_subset, me * OWN, OWN, 0)
    gaps = jnp.take(occ_gap, own_subset)
    so_far, gaps = lax.optimization_barrier((so_far, gaps))
    mine, away = tail(near[3], far[3], p4, so_far)
    other = permute(away, perm=across_core())
    dealt = deal(me[None], mine, other)
    terms = [dealt[0]]
    for step in (3, 2, 1):
        terms.append(lax.ppermute(dealt[step], "grp", [(i, i ^ step) for i in range(GRP)]))
    return close(terms, gaps[:, None], vir_energy[None, :])


def solution(mesh):
    return jax.shard_map(
        body,
        mesh=mesh,
        in_specs=(P(None, "grp", "blk"), P("grp", "blk"), P(), P(), P("blk"), P()),
        out_specs=P("grp", "blk"),
        check_vma=False,
    )
```

time: 118 us -> 108 us (0.915)
  blocking collectives: 22.8 us -> 0 us
  waiting for transfers between devices: 14.8 us -> 25.9 us
  Pallas kernels: 7.78 us -> 13.1 us
  starting transfers between devices: 60.9 us -> 56.8 us
  local copies, waits for them, and re-layouts: 7.39 us -> 10.1 us
    all_to_all x1 -> x0, blocking collectives: 22.8 us -> none  [body(): lax.all_to_all(copies, 'blk', 0, 0, axis_index_groups=groups(), tiled=True)]
    ppermute x10 -> x9, starting transfers between devices: 45.1 us -> 36.3 us  [the longest x3 10 us: body(): lax.ppermute(dealt[step], 'grp', [(i, i ^ step) for i in range(GRP)])]
    unnamed x18 -> x42, local copies, waits for them, and re-layouts: 1.63 us -> 8.72 us
    ppermute x1, waiting for transfers between devices: 0.01 us -> 5.71 us  [body(): across = permute(own, perm=across_h())]
    all_to_all x0 -> x1, waiting for transfers between devices: none -> 5.17 us  [body(): lax.all_to_all(copies, 'blk', 0, 0, axis_index_groups=groups(), tiled=True)]
    all_to_all x0 -> x1, starting transfers between devices: none -> 4.67 us  [body(): lax.all_to_all(copies, 'blk', 0, 0, axis_index_groups=groups(), tiled=True)]
    pallas_call x1 -> x8, Pallas kernels: 6.61 us -> 11 us  [the longest x3 5.11 us: early(): pl.pallas_call(functools.partial(early_kernel, len(pieces), before is Non...]
    dynamic_slice x1 -> x0, local copies, waits for them, and re-layouts: 3.15 us -> none  [body(): lax.dynamic_index_in_dim(pairs, 1 - c, axis=1, keepdims=False)]
  transfers between devices with their start and end apart: 14 -> 14, of which waited for: 5 -> 6; matrix products, arithmetic and copies ran while one was open for 6% -> 2% of each run, Pallas kernels for 0% -> 10%
where the time goes in v2:
time: 108 us; the launch traced here: 107 us
  starting transfers between devices  56.8 us (53%)
  waiting for transfers between devices  25.9 us (24%)
  Pallas kernels  13.1 us (12%)
  local copies, waits for them, and re-layouts  10.1 us (9%)
    ppermute x3, starting transfers between devices, body(): lax.ppermute(dealt[step], 'grp', [(i, i ^ step) for i in range(GRP)])  10 us
    ppermute x1, starting transfers between devices, body(): got = permute(ints, perm=across_core())  8.79 us
    unnamed x42, local copies, waits for them, and re-layouts  8.72 us
    ppermute x1, starting transfers between devices, body(): other = permute(away, perm=across_core())  8.4 us
    ppermute x1, starting transfers between devices, body(): across = permute(own, perm=across_h())  7.45 us
    ppermute x3, waiting for transfers between devices, body(): lax.ppermute(dealt[step], 'grp', [(i, i ^ step) for i in range(GRP)])  7.44 us
    ppermute x1, waiting for transfers between devices, body(): across = permute(own, perm=across_h())  5.71 us
    all_to_all x1, waiting for transfers between devices, body(): lax.all_to_all(copies, 'blk', 0, 0, axis_index_groups=groups(), tiled=True)  5.17 us
  transfers between devices with their start and end apart: 14, of which 6 were waited for; matrix products, arithmetic and copies ran while one was open for 2% of the time, Pallas kernels for 10%

profile of v2, /device:TPU:1, one launch (start us, length us, event | category | flops | bytes accessed | tf_op | source)
XLA Modules:
  0.0 107.2 jit_solution(15851553223759401975)
XLA Ops:
  0.0 0.0 copy-start
  0.0 0.9 copy-done.16
  0.9 0.7 copy-done.17
  1.6 1.3 %select.55 = bf16[512,512]{1,0:T(8,128)(2,1)} custom-call(bf16[64,1024]{1,0:T(8,128)(2,1)S(1)} %bitcast.17, s32[1,512]{1,0:T(1,128)S(1)} %bitcast.18), custom_call_target="tpu_custom_call" | custom-call | tf_op jit(solution)/shard_map/select/pallas_call | solution.py:74
  2.9 8.8 %collective-permute-start = (bf16[8192,256]{1,0:T(8,128)(2,1)}, bf16[8192,256]{1,0:T(8,128)(2,1)}, u32[]{:S(2)}, u32[]{:S(2)}) collective-permute-start(bf16[8192,256]{1,0:T(8,128)(2,1)} %ints_ref.1), channel_id=1, source_target_pairs={{0,4},{4,0},{8,12},{12,8},{16,20},{20,16},{24,28},{28,24},{32,36},... | collective-permute-start | bytes 12582920 | tf_op jit(solution)/shard_map/ppermute | solution.py:239
  11.7 4.7 %all-to-all-start = ((bf16[8,64,512]{2,1,0:T(8,128)(2,1)}), bf16[8,64,512]{2,1,0:T(8,128)(2,1)S(1)}, u32[]{:S(2)}, u32[]{:S(2)}) async-start(bf16[8,64,512]{2,1,0:T(8,128)(2,1)} %bitcast.4), calls=%async_computation | async-start | bytes 1048576 | tf_op jit(solution)/shard_map/all_to_all | solution.py:257
  16.5 0.1 concatenate.13
  16.6 0.1 concatenate.12
  16.7 0.1 fusion.1
  16.8 0.1 pad_add_fusion.1.place_ref
  16.8 0.4 convert_reduce_fusion
  17.2 0.1 fusion.4
  17.3 0.1 select_reduce_fusion
  17.4 0.0 copy-start.1
  17.4 2.2 %copy-done.1 = bf16[8192,256]{1,0:T(8,128)(2,1)S(1)} copy-done((bf16[8192,256]{1,0:T(8,128)(2,1)S(1)}, bf16[8192,256]{1,0:T(8,128)(2,1)}, u32[]{:S(2)}) %copy-start.1) | copy-done | bytes 4194328
  19.6 1.4 %prepare.2 = (bf16[3,256,512]{2,1,0:T(8,128)(2,1)S(1)}, bf16[2,256,512]{2,1,0:T(8,128)(2,1)S(1)}, bf16[2,256,512]{2,1,0:T(8,128)(2,1)S(1)}, bf16[1,256,512]{2,1,0:T(8,128)(2,1)S(1)}) custom-call(s32[66]{0:T(128)S(1)} %pad_add_fusion.1.place_ref, bf16[8192,256]{1,0:T(8,128)(2,1)S(1)} %copy-done.1, s32[1,256]{1,0:T(1,128)S(1)} %get-tuple-element.83.low_ref, ...), custom_call_target="tpu_custom_call" | custom-call | bytes 12582912 | tf_op jit(solution)/shard_map/prepare/pallas_call | solution.py:132
  21.0 0.8 copy-done.2
  21.8 0.8 copy-done.4
  22.7 0.7 copy-done.12
  23.4 5.2 %all-to-all-done = bf16[8,64,512]{2,1,0:T(8,128)(2,1)S(1)} async-done(((bf16[8,64,512]{2,1,0:T(8,128)(2,1)}), bf16[8,64,512]{2,1,0:T(8,128)(2,1)S(1)}, u32[]{:S(2)}, u32[]{:S(2)}) %all-to-all-start) | async-done | bytes 524320 | tf_op jit(solution)/shard_map/all_to_all | solution.py:257
  28.6 3.1 %collective-permute-start.1 = (bf16[512,512]{1,0:T(8,128)(2,1)S(1)}, bf16[512,512]{1,0:T(8,128)(2,1)S(1)}, u32[]{:S(2)}, u32[]{:S(2)}) collective-permute-start(bf16[512,512]{1,0:T(8,128)(2,1)S(1)} %bitcast.13), channel_id=1, source_target_pairs={{0,32},{4,12},{8,40},{12,20},{16,48},{20,28},{24,56},{28,4},{32,64... | collective-permute-start | bytes 1572872 | tf_op jit(solution)/shard_map/ppermute | solution.py:261
  31.7 3.4 %collective-permute-start.5 = (bf16[512,512]{1,0:T(8,128)(2,1)S(1)}, bf16[512,512]{1,0:T(8,128)(2,1)}, u32[]{:S(2)}, u32[]{:S(2)}) collective-permute-start(bf16[512,512]{1,0:T(8,128)(2,1)S(1)} %bitcast.14), channel_id=1, source_target_pairs={{0,224},{4,28},{8,232},{12,4},{16,240},{20,12},{24,248},{28,20},{3... | collective-permute-start | bytes 1572872 | tf_op jit(solution)/shard_map/ppermute | solution.py:262
  35.0 7.5 %collective-permute-start.3 = (bf16[512,512]{1,0:T(8,128)(2,1)S(1)}, bf16[512,512]{1,0:T(8,128)(2,1)S(1)}, u32[]{:S(2)}, u32[]{:S(2)}) collective-permute-start(bf16[512,512]{1,0:T(8,128)(2,1)S(1)} %bitcast.15), channel_id=1, source_target_pairs={{4,260},{12,268},{20,276},{28,284},{36,292},{44,300},{52,308},{60,... | collective-permute-start | bytes 1572872 | tf_op jit(solution)/shard_map/ppermute | solution.py:263
  42.5 0.0 collective-permute-done.1.refs_1_
  42.5 0.0 copy-start.6
  42.5 1.9 %collective-permute-start.2 = (bf16[512,512]{1,0:T(8,128)(2,1)S(1)}, bf16[512,512]{1,0:T(8,128)(2,1)S(1)}, u32[]{:S(2)}, u32[]{:S(2)}) collective-permute-start(bf16[512,512]{1,0:T(8,128)(2,1)S(1)} %collective-permute-done.1.refs_1_), channel_id=1, source_target_pairs={{0,32},{4,12},{8,40},{12,20},{16,48},{20,28},{24,56},{28,4},{32,64... | collective-permute-start | bytes 1572872 | tf_op jit(solution)/shard_map/ppermute | solution.py:265
  44.5 0.0 collective-permute-done.5.refs_2_
  44.5 0.7 collective-permute-start.7
  45.2 5.7 %collective-permute-done.3.second_ref = bf16[512,512]{1,0:T(8,128)(2,1)S(1)} collective-permute-done((bf16[512,512]{1,0:T(8,128)(2,1)S(1)}, bf16[512,512]{1,0:T(8,128)(2,1)S(1)}, u32[]{:S(2)}, u32[]{:S(2)}) %collective-permute-start.3) | collective-permute-done | bytes 524320 | tf_op jit(solution)/shard_map/ppermute | solution.py:263
  50.9 3.1 %collective-permute-done.2.first_ref.refs_0_ = bf16[512,512]{1,0:T(8,128)(2,1)S(1)} collective-permute-done((bf16[512,512]{1,0:T(8,128)(2,1)S(1)}, bf16[512,512]{1,0:T(8,128)(2,1)S(1)}, u32[]{:S(2)}, u32[]{:S(2)}) %collective-permute-start.2) | collective-permute-done | bytes 524320 | tf_op jit(solution)/shard_map/ppermute | solution.py:265
  54.0 0.8 pick.2
  54.8 1.9 %collective-permute-start.4 = (bf16[512,512]{1,0:T(8,128)(2,1)}, bf16[512,512]{1,0:T(8,128)(2,1)}, u32[]{:S(2)}, u32[]{:S(2)}) collective-permute-start(bf16[512,512]{1,0:T(8,128)(2,1)} %pick.2), channel_id=1, source_target_pairs={{0,32},{4,12},{8,40},{12,20},{16,48},{20,28},{24,56},{28,4},{32,64... | collective-permute-start | bytes 1572872 | tf_op jit(solution)/shard_map/ppermute | solution.py:270
  56.7 0.0 collective-permute-done.7.first_ref
  56.8 4.6 %collective-permute-start.8 = (bf16[512,512]{1,0:T(8,128)(2,1)S(1)}, bf16[512,512]{1,0:T(8,128)(2,1)}, u32[]{:S(2)}, u32[]{:S(2)}) collective-permute-start(bf16[512,512]{1,0:T(8,128)(2,1)S(1)} %pick.3.refs_1_), channel_id=1, source_target_pairs={{0,224},{4,28},{8,232},{12,4},{16,240},{20,12},{24,248},{28,20},{3... | collective-permute-start | bytes 1572872 | tf_op jit(solution)/shard_map/ppermute | solution.py:272
  61.4 0.0 collective-permute-done.ints_ref
  61.4 3.1 %prepare.3 = (bf16[3,256,512]{2,1,0:T(8,128)(2,1)S(1)}, bf16[2,256,512]{2,1,0:T(8,128)(2,1)S(1)}, bf16[2,256,512]{2,1,0:T(8,128)(2,1)S(1)}, bf16[1,256,512]{2,1,0:T(8,128)(2,1)S(1)}) custom-call(s32[66]{0:T(128)S(1)} %pad_add_fusion.1.place_ref, bf16[8192,256]{1,0:T(8,128)(2,1)} %collective-permute-done.ints_ref, s32[1,256]{1,0:T(1,128)S(1)} %get-tuple-element.84.low_ref, ...), custom_call_target="tpu_custom_call" | custom-call | bytes 12582912 | tf_op jit(solution)/shard_map/prepare/pallas_call | solution.py:132
  64.6 0.0 copy-start.18
  64.6 2.4 %early.3.refs_2_ = f32[512,512]{1,0:T(8,128)S(1)} custom-call(bf16[3,256,512]{2,1,0:T(8,128)(2,1)S(1)} %get-tuple-element.41.near_ref, bf16[3,256,512]{2,1,0:T(8,128)(2,1)S(1)} %get-tuple-element.42.far_ref, bf16[512,512]{1,0:T(8,128)(2,1)S(1)} %bitcast.16, bf16[512,512]{1,0:T(8,128)(2,1)S(1)} %copy-done.7, bf16[512,512]{1,0:T(8,128)(2,1)} %collective-permute-done.5.refs_2_), custom_call_target="tpu_custom_call" | custom-call | flops 805306368 | bytes 3145728 | tf_op jit(solution)/shard_map/early/pallas_call | solution.py:157
  67.1 0.0 collective-permute-done.4.refs_0_
  67.1 1.9 %collective-permute-start.6 = (bf16[512,512]{1,0:T(8,128)(2,1)}, bf16[512,512]{1,0:T(8,128)(2,1)S(1)}, u32[]{:S(2)}, u32[]{:S(2)}) collective-permute-start(bf16[512,512]{1,0:T(8,128)(2,1)} %collective-permute-done.4.refs_0_), channel_id=1, source_target_pairs={{0,32},{4,12},{8,40},{12,20},{16,48},{20,28},{24,56},{28,4},{32,64... | collective-permute-start | bytes 1572872 | tf_op jit(solution)/shard_map/ppermute | solution.py:274
  69.0 0.1 compare_select_fusion
  69.1 1.0 gather_fusion
  70.1 0.1 and_select_fusion
  70.2 1.0 copy-done.5
  71.2 1.0 copy-done.11
  72.3 0.7 early.4.refs_2_
  73.0 0.0 collective-permute-done.8.refs_1_
  73.0 0.3 copy-done.3
  73.3 0.2 copy-done.9
  73.5 2.0 %early.5.before_ref = f32[512,512]{1,0:T(8,128)S(1)} custom-call(bf16[2,256,512]{2,1,0:T(8,128)(2,1)S(1)} %copy-done.3, bf16[2,256,512]{2,1,0:T(8,128)(2,1)S(1)} %copy-done.9, bf16[512,512]{1,0:T(8,128)(2,1)} %collective-permute-done.4.refs_0_, bf16[512,512]{1,0:T(8,128)(2,1)} %collective-permute-done.8.refs_1_, f32[512,512]{1,0:T(8,128)S(1)} %early.4.refs_2_), custom_call_target="tpu_custom_call" | custom-call | flops 536870912 | bytes 2097152 | tf_op jit(solution)/shard_map/early/pallas_call | solution.py:157
  75.4 0.0 copy-start.19
  75.4 3.0 %collective-permute-done.6.piece_ref = bf16[512,512]{1,0:T(8,128)(2,1)S(1)} collective-permute-done((bf16[512,512]{1,0:T(8,128)(2,1)}, bf16[512,512]{1,0:T(8,128)(2,1)S(1)}, u32[]{:S(2)}, u32[]{:S(2)}) %collective-permute-start.6) | collective-permute-done | bytes 524320 | tf_op jit(solution)/shard_map/ppermute | solution.py:274
  78.4 0.4 tail.1
  78.9 8.4 %collective-permute-start.9 = (f32[4,256,128]{2,1,0:T(8,128)S(1)}, f32[4,256,128]{2,1,0:T(8,128)S(1)}, u32[]{:S(2)}, u32[]{:S(2)}) collective-permute-start(f32[4,256,128]{2,1,0:T(8,128)S(1)} %get-tuple-element.51), channel_id=1, source_target_pairs={{0,4},{4,0},{8,12},{12,8},{16,20},{20,16},{24,28},{28,24},{32,36},... | collective-permute-start | bytes 1572872 | tf_op jit(solution)/shard_map/ppermute | solution.py:280
  87.3 1.5 %collective-permute-done.9.other_ref = f32[4,256,128]{2,1,0:T(8,128)S(1)} collective-permute-done((f32[4,256,128]{2,1,0:T(8,128)S(1)}, f32[4,256,128]{2,1,0:T(8,128)S(1)}, u32[]{:S(2)}, u32[]{:S(2)}) %collective-permute-start.9) | collective-permute-done | bytes 524320 | tf_op jit(solution)/shard_map/ppermute | solution.py:280
  88.8 0.1 deal.1
  88.9 3.2 %collective-permute-start.10 = (f32[256,128]{1,0:T(8,128)S(1)}, f32[256,128]{1,0:T(8,128)S(1)}, u32[]{:S(2)}, u32[]{:S(2)}) collective-permute-start(f32[256,128]{1,0:T(8,128)S(1)} %get-tuple-element.53), channel_id=1, source_target_pairs={{0,3},{1,2},{2,1},{3,0},{4,7},{5,6},{6,5},{7,4},{8,11},{9,10},{10,... | collective-permute-start | bytes 393224 | tf_op jit(solution)/shard_map/ppermute | solution.py:284
  92.0 4.9 %collective-permute-start.11 = (f32[256,128]{1,0:T(8,128)S(1)}, f32[256,128]{1,0:T(8,128)S(1)}, u32[]{:S(2)}, u32[]{:S(2)}) collective-permute-start(f32[256,128]{1,0:T(8,128)S(1)} %get-tuple-element.54), channel_id=1, source_target_pairs={{0,2},{1,3},{2,0},{3,1},{4,6},{5,7},{6,4},{7,5},{8,10},{9,11},{10,... | collective-permute-start | bytes 393224 | tf_op jit(solution)/shard_map/ppermute | solution.py:284
  97.0 1.9 %collective-permute-start.12 = (f32[256,128]{1,0:T(8,128)S(1)}, f32[256,128]{1,0:T(8,128)S(1)}, u32[]{:S(2)}, u32[]{:S(2)}) collective-permute-start(f32[256,128]{1,0:T(8,128)S(1)} %get-tuple-element.55), channel_id=1, source_target_pairs={{0,1},{1,0},{2,3},{3,2},{4,5},{5,4},{6,7},{7,6},{8,9},{9,8},{10,11... | collective-permute-start | bytes 393224 | tf_op jit(solution)/shard_map/ppermute | solution.py:284
  98.9 0.1 copy.9.gap_ref
  99.0 0.0 collective-permute-done.10.b_ref
  99.0 7.4 %collective-permute-done.11.c_ref = f32[256,128]{1,0:T(8,128)S(1)} collective-permute-done((f32[256,128]{1,0:T(8,128)S(1)}, f32[256,128]{1,0:T(8,128)S(1)}, u32[]{:S(2)}, u32[]{:S(2)}) %collective-permute-start.11) | collective-permute-done | bytes 131104 | tf_op jit(solution)/shard_map/ppermute | solution.py:284
  106.5 0.0 collective-permute-done.12.d_ref
  106.5 0.8 close.1
  (40 shorter events, 0.2 us)
Async XLA Ops:
  0.0 69.1 %copy-start = (f32[1024]{0:T(1024)S(1)}, f32[1024]{0:T(1024)}, u32[]{:S(2)}) copy-start(f32[1024]{0:T(1024)} %param.9) | copy-start | bytes 12292
  0.0 0.9 copy-start.16
  0.9 0.7 copy-start.17
  1.6 15.1 %copy-start.20 = (s32[32768]{0:T(1024)S(1)}, s32[32768]{0:T(1024)}, u32[]{:S(2)}) copy-start(s32[32768]{0:T(1024)} %param.8) | copy-start | bytes 393220
  2.9 58.4 %collective-permute-start = (bf16[8192,256]{1,0:T(8,128)(2,1)}, bf16[8192,256]{1,0:T(8,128)(2,1)}, u32[]{:S(2)}, u32[]{:S(2)}) collective-permute-start(bf16[8192,256]{1,0:T(8,128)(2,1)} %ints_ref.1), channel_id=1, source_target_pairs={{0,4},{4,0},{8,12},{12,8},{16,20},{20,16},{24,28},{28,24},{32,36},... | collective-permute-start | bytes 12582920 | tf_op jit(solution)/shard_map/ppermute | solution.py:239
  11.7 16.8 %all-to-all-start = ((bf16[8,64,512]{2,1,0:T(8,128)(2,1)}), bf16[8,64,512]{2,1,0:T(8,128)(2,1)S(1)}, u32[]{:S(2)}, u32[]{:S(2)}) async-start(bf16[8,64,512]{2,1,0:T(8,128)(2,1)} %bitcast.4), calls=%async_computation | async-start | bytes 1048576 | tf_op jit(solution)/shard_map/all_to_all | solution.py:257
  17.4 2.2 %copy-start.1 = (bf16[8192,256]{1,0:T(8,128)(2,1)S(1)}, bf16[8192,256]{1,0:T(8,128)(2,1)}, u32[]{:S(2)}) copy-start(bf16[8192,256]{1,0:T(8,128)(2,1)} %ints_ref.1) | copy-start | bytes 12582916
  21.0 0.8 copy-start.2
  21.8 0.8 copy-start.4
  22.7 0.7 copy-start.12
  28.6 14.0 %collective-permute-start.1 = (bf16[512,512]{1,0:T(8,128)(2,1)S(1)}, bf16[512,512]{1,0:T(8,128)(2,1)S(1)}, u32[]{:S(2)}, u32[]{:S(2)}) collective-permute-start(bf16[512,512]{1,0:T(8,128)(2,1)S(1)} %bitcast.13), channel_id=1, source_target_pairs={{0,32},{4,12},{8,40},{12,20},{16,48},{20,28},{24,56},{28,4},{32,64... | collective-permute-start | bytes 1572872 | tf_op jit(solution)/shard_map/ppermute | solution.py:261
  31.7 12.8 %collective-permute-start.5 = (bf16[512,512]{1,0:T(8,128)(2,1)S(1)}, bf16[512,512]{1,0:T(8,128)(2,1)}, u32[]{:S(2)}, u32[]{:S(2)}) collective-permute-start(bf16[512,512]{1,0:T(8,128)(2,1)S(1)} %bitcast.14), channel_id=1, source_target_pairs={{0,224},{4,28},{8,232},{12,4},{16,240},{20,12},{24,248},{28,20},{3... | collective-permute-start | bytes 1572872 | tf_op jit(solution)/shard_map/ppermute | solution.py:262
  35.0 15.8 %collective-permute-start.3 = (bf16[512,512]{1,0:T(8,128)(2,1)S(1)}, bf16[512,512]{1,0:T(8,128)(2,1)S(1)}, u32[]{:S(2)}, u32[]{:S(2)}) collective-permute-start(bf16[512,512]{1,0:T(8,128)(2,1)S(1)} %bitcast.15), channel_id=1, source_target_pairs={{4,260},{12,268},{20,276},{28,284},{36,292},{44,300},{52,308},{60,... | collective-permute-start | bytes 1572872 | tf_op jit(solution)/shard_map/ppermute | solution.py:263
  42.5 14.2 %copy-start.6 = (bf16[512,512]{1,0:T(8,128)(2,1)}, bf16[512,512]{1,0:T(8,128)(2,1)S(1)}, u32[]{:S(2)}) copy-start(bf16[512,512]{1,0:T(8,128)(2,1)S(1)} %collective-permute-done.1.refs_1_) | copy-start | bytes 1572868
  42.5 11.4 %collective-permute-start.2 = (bf16[512,512]{1,0:T(8,128)(2,1)S(1)}, bf16[512,512]{1,0:T(8,128)(2,1)S(1)}, u32[]{:S(2)}, u32[]{:S(2)}) collective-permute-start(bf16[512,512]{1,0:T(8,128)(2,1)S(1)} %collective-permute-done.1.refs_1_), channel_id=1, source_target_pairs={{0,32},{4,12},{8,40},{12,20},{16,48},{20,28},{24,56},{28,4},{32,64... | collective-permute-start | bytes 1572872 | tf_op jit(solution)/shard_map/ppermute | solution.py:265
  44.5 12.3 %collective-permute-start.7 = (bf16[512,512]{1,0:T(8,128)(2,1)}, bf16[512,512]{1,0:T(8,128)(2,1)S(1)}, u32[]{:S(2)}, u32[]{:S(2)}) collective-permute-start(bf16[512,512]{1,0:T(8,128)(2,1)} %collective-permute-done.5.refs_2_), channel_id=1, source_target_pairs={{0,224},{8,232},{16,240},{24,248},{32,0},{40,8},{48,16},{56,24},{6... | collective-permute-start | bytes 1572872 | tf_op jit(solution)/shard_map/ppermute | solution.py:266
  54.8 12.3 %collective-permute-start.4 = (bf16[512,512]{1,0:T(8,128)(2,1)}, bf16[512,512]{1,0:T(8,128)(2,1)}, u32[]{:S(2)}, u32[]{:S(2)}) collective-permute-start(bf16[512,512]{1,0:T(8,128)(2,1)} %pick.2), channel_id=1, source_target_pairs={{0,32},{4,12},{8,40},{12,20},{16,48},{20,28},{24,56},{28,4},{32,64... | collective-permute-start | bytes 1572872 | tf_op jit(solution)/shard_map/ppermute | solution.py:270
  56.8 16.2 %collective-permute-start.8 = (bf16[512,512]{1,0:T(8,128)(2,1)S(1)}, bf16[512,512]{1,0:T(8,128)(2,1)}, u32[]{:S(2)}, u32[]{:S(2)}) collective-permute-start(bf16[512,512]{1,0:T(8,128)(2,1)S(1)} %pick.3.refs_1_), channel_id=1, source_target_pairs={{0,224},{4,28},{8,232},{12,4},{16,240},{20,12},{24,248},{28,20},{3... | collective-permute-start | bytes 1572872 | tf_op jit(solution)/shard_map/ppermute | solution.py:272
  61.4 3.2 %copy-start.7 = (bf16[512,512]{1,0:T(8,128)(2,1)S(1)}, bf16[512,512]{1,0:T(8,128)(2,1)}, u32[]{:S(2)}) copy-start(bf16[512,512]{1,0:T(8,128)(2,1)} %copy-done.6) | copy-start | bytes 1572868
  64.5 2.5 %copy-start.8 = (bf16[2,256,512]{2,1,0:T(8,128)(2,1)}, bf16[2,256,512]{2,1,0:T(8,128)(2,1)S(1)}, u32[]{:S(2)}) copy-start(bf16[2,256,512]{2,1,0:T(8,128)(2,1)S(1)} %get-tuple-element.45.far_ref) | copy-start | bytes 1572868
  64.5 2.5 %copy-start.10 = (bf16[2,256,512]{2,1,0:T(8,128)(2,1)}, bf16[2,256,512]{2,1,0:T(8,128)(2,1)S(1)}, u32[]{:S(2)}) copy-start(bf16[2,256,512]{2,1,0:T(8,128)(2,1)S(1)} %get-tuple-element.47.far_ref) | copy-start | bytes 1572868
  64.6 2.5 %copy-start.14 = (bf16[1,256,512]{2,1,0:T(8,128)(2,1)}, bf16[1,256,512]{2,1,0:T(8,128)(2,1)S(1)}, u32[]{:S(2)}) copy-start(bf16[1,256,512]{2,1,0:T(8,128)(2,1)S(1)} %get-tuple-element.39.far_ref) | copy-start | bytes 786436
  64.6 4.4 %copy-start.18 = (s32[512]{0:T(512)S(1)}, s32[512]{0:T(512)}, u32[]{:S(2)}) copy-start(s32[512]{0:T(512)} %param.11) | copy-start | bytes 6148
  67.1 11.3 %collective-permute-start.6 = (bf16[512,512]{1,0:T(8,128)(2,1)}, bf16[512,512]{1,0:T(8,128)(2,1)S(1)}, u32[]{:S(2)}, u32[]{:S(2)}) collective-permute-start(bf16[512,512]{1,0:T(8,128)(2,1)} %collective-permute-done.4.refs_0_), channel_id=1, source_target_pairs={{0,32},{4,12},{8,40},{12,20},{16,48},{20,28},{24,56},{28,4},{32,64... | collective-permute-start | bytes 1572872 | tf_op jit(solution)/shard_map/ppermute | solution.py:274
  70.2 1.0 copy-start.5
  71.2 1.0 copy-start.11
  72.3 1.0 copy-start.3
  72.3 1.2 %copy-start.9 = (bf16[2,256,512]{2,1,0:T(8,128)(2,1)S(1)}, bf16[2,256,512]{2,1,0:T(8,128)(2,1)}, u32[]{:S(2)}) copy-start(bf16[2,256,512]{2,1,0:T(8,128)(2,1)} %copy-done.8) | copy-start | bytes 1572868
  73.5 5.0 %copy-start.13 = (bf16[1,256,512]{2,1,0:T(8,128)(2,1)S(1)}, bf16[1,256,512]{2,1,0:T(8,128)(2,1)}, u32[]{:S(2)}) copy-start(bf16[1,256,512]{2,1,0:T(8,128)(2,1)} %copy-done.12) | copy-start | bytes 786436
  73.5 5.0 %copy-start.15 = (bf16[1,256,512]{2,1,0:T(8,128)(2,1)S(1)}, bf16[1,256,512]{2,1,0:T(8,128)(2,1)}, u32[]{:S(2)}) copy-start(bf16[1,256,512]{2,1,0:T(8,128)(2,1)} %copy-done.14) | copy-start | bytes 786436
  75.4 31.0 %copy-start.19 = (f32[256]{0:T(256)S(1)}, f32[256]{0:T(256)}, u32[]{:S(2)}) copy-start(f32[256]{0:T(256)} %param.10) | copy-start | bytes 3076
  78.9 9.9 %collective-permute-start.9 = (f32[4,256,128]{2,1,0:T(8,128)S(1)}, f32[4,256,128]{2,1,0:T(8,128)S(1)}, u32[]{:S(2)}, u32[]{:S(2)}) collective-permute-start(f32[4,256,128]{2,1,0:T(8,128)S(1)} %get-tuple-element.51), channel_id=1, source_target_pairs={{0,4},{4,0},{8,12},{12,8},{16,20},{20,16},{24,28},{28,24},{32,36},... | collective-permute-start | bytes 1572872 | tf_op jit(solution)/shard_map/ppermute | solution.py:280
  88.9 10.2 %collective-permute-start.10 = (f32[256,128]{1,0:T(8,128)S(1)}, f32[256,128]{1,0:T(8,128)S(1)}, u32[]{:S(2)}, u32[]{:S(2)}) collective-permute-start(f32[256,128]{1,0:T(8,128)S(1)} %get-tuple-element.53), channel_id=1, source_target_pairs={{0,3},{1,2},{2,1},{3,0},{4,7},{5,6},{6,5},{7,4},{8,11},{9,10},{10,... | collective-permute-start | bytes 393224 | tf_op jit(solution)/shard_map/ppermute | solution.py:284
  92.0 14.4 %collective-permute-start.11 = (f32[256,128]{1,0:T(8,128)S(1)}, f32[256,128]{1,0:T(8,128)S(1)}, u32[]{:S(2)}, u32[]{:S(2)}) collective-permute-start(f32[256,128]{1,0:T(8,128)S(1)} %get-tuple-element.54), channel_id=1, source_target_pairs={{0,2},{1,3},{2,0},{3,1},{4,6},{5,7},{6,4},{7,5},{8,10},{9,11},{10,... | collective-permute-start | bytes 393224 | tf_op jit(solution)/shard_map/ppermute | solution.py:284
  97.0 9.5 %collective-permute-start.12 = (f32[256,128]{1,0:T(8,128)S(1)}, f32[256,128]{1,0:T(8,128)S(1)}, u32[]{:S(2)}, u32[]{:S(2)}) collective-permute-start(f32[256,128]{1,0:T(8,128)S(1)} %get-tuple-element.55), channel_id=1, source_target_pairs={{0,1},{1,0},{2,3},{3,2},{4,5},{5,4},{6,7},{7,6},{8,9},{9,8},{10,11... | collective-permute-start | bytes 393224 | tf_op jit(solution)/shard_map/ppermute | solution.py:284

commit v3 on v2

--- a/solution.py
+++ b/solution.py
@@ -14,8 +14,8 @@
 COLS = 256
 GRP = 4
 OWN = OCC // GRP
-VMEM_LIMIT = 16 * 1024 * 1024
-STAGES = ((0, 1, 2), (3, 4), (5, 6), (7,))
+VMEM_LIMIT = 12 * 1024 * 1024
+STAGES = ((0, 1, 2), (3, 5), (6, 7), (4,))
 
 
 def index(h, z, x, c):
@@ -41,15 +41,19 @@
     return pairs
 
 
-def across_h():
-    return [(index(h, z, x, 1), index(h + 1, z, x, 1)) for h, z, x, c in devices() if c == 1]
+def across():
+    pairs = []
+    for h, z, x, c in devices():
+        target = index(h, z + 4, x, 0) if c == 0 else index(h + 1, z, x, 1)
+        pairs.append((index(h, z, x, c), target))
+    return pairs
 
 
 def across_core():
     return [(index(h, z, x, c), index(h, z, x, 1 - c)) for h, z, x, c in devices()]
 
 
-def select_kernel(amp_ref, subset_ref, out_ref, held_ref, amp_here, subset_here, sems):
+def select_kernel(amp_ref, subset_ref, out_ref, copies_ref, amp_here, subset_here, sems):
     fetch = [
         pltpu.make_async_copy(amp_ref, amp_here, sems.at[8]),
         pltpu.make_async_copy(subset_ref, subset_here, sems.at[9]),
@@ -60,9 +64,33 @@
         copy.wait()
     rows = amp_here.shape[1]
     hot = (lax.broadcasted_iota(jnp.int32, (rows, OCC), 0) == subset_here[...]).astype(jnp.bfloat16)
-    held_ref[...] = jnp.dot(amp_here[...], hot, preferred_element_type=jnp.float32).astype(jnp.bfloat16)
+    out_ref[...] = jnp.dot(amp_here[...], hot, preferred_element_type=jnp.float32).astype(jnp.bfloat16)
+    send_copies(out_ref, copies_ref, sems)
+
+
+def select(amplitudes, subset):
+    hbm, vmem = pl.BlockSpec(memory_space=pltpu.HBM), pl.BlockSpec(memory_space=pltpu.VMEM)
+    return pl.pallas_call(
+        select_kernel,
+        out_shape=[
+            jax.ShapeDtypeStruct((SHARD, OCC), jnp.bfloat16),
+            jax.ShapeDtypeStruct((8 * SHARD, OCC), jnp.bfloat16),
+        ],
+        in_specs=[hbm, hbm],
+        out_specs=[vmem, hbm],
+        scratch_shapes=[
+            pltpu.VMEM(amplitudes.shape, amplitudes.dtype),
+            pltpu.VMEM(subset.shape, subset.dtype),
+            pltpu.SemaphoreType.DMA((10,)),
+        ],
+        compiler_params=pltpu.CompilerParams(vmem_limit_bytes=VMEM_LIMIT),
+        name="select",
+    )(pltpu.with_memory_space_constraint(amplitudes, pltpu.HBM), pltpu.with_memory_space_constraint(subset, pltpu.HBM))
+
+
+def send_copies(shard_ref, out_ref, sems):
     copies = [
-        pltpu.make_async_copy(held_ref, out_ref.at[pl.ds(copy * SHARD, SHARD), :], sems.at[copy]) for copy in range(8)
+        pltpu.make_async_copy(shard_ref, out_ref.at[pl.ds(copy * SHARD, SHARD), :], sems.at[copy]) for copy in range(8)
     ]
     for copy in copies:
         copy.start()
@@ -70,21 +98,20 @@
         copy.wait()
 
 
-def select(amplitudes, subset):
-    return pl.pallas_call(
-        select_kernel,
+def spread_kernel(shard_ref, out_ref, sems):
+    send_copies(shard_ref, out_ref, sems)
+
+
+def spread(shard):
+    return pl.pallas_call(
+        spread_kernel,
         out_shape=jax.ShapeDtypeStruct((8 * SHARD, OCC), jnp.bfloat16),
-        in_specs=[pl.BlockSpec(memory_space=pltpu.HBM)] * 2,
+        in_specs=[pl.BlockSpec(memory_space=pltpu.VMEM)],
         out_specs=pl.BlockSpec(memory_space=pltpu.HBM),
-        scratch_shapes=[
-            pltpu.VMEM((SHARD, OCC), jnp.bfloat16),
-            pltpu.VMEM(amplitudes.shape, amplitudes.dtype),
-            pltpu.VMEM(subset.shape, subset.dtype),
-            pltpu.SemaphoreType.DMA((10,)),
-        ],
-        compiler_params=pltpu.CompilerParams(vmem_limit_bytes=VMEM_LIMIT),
-        name="select",
-    )(amplitudes, subset)
+        scratch_shapes=[pltpu.SemaphoreType.DMA((8,))],
+        compiler_params=pltpu.CompilerParams(vmem_limit_bytes=VMEM_LIMIT),
+        name="spread",
+    )(shard)
 
 
 def pick_kernel(core_ref, first_ref, second_ref, out_ref):
@@ -109,22 +136,24 @@
     )(core, first, second)
 
 
-def prepare_kernel(place_ref, ints_ref, low_ref, high_ref, *out_refs):
+def prepare_kernel(place_ref, ints_ref, low_ref, high_ref, *refs):
+    out_refs, held_ref, sem = refs[: len(STAGES)], refs[-2], refs[-1]
     core = place_ref[64]
     start = place_ref[65]
+    fetch = pltpu.make_async_copy(ints_ref.at[:, core], held_ref, sem)
+    fetch.start()
+    fetch.wait()
     low, high = low_ref[...], high_ref[...]
-    for number in range(8):
-        parts = []
-        for chunk in range(8):
-            shard = place_ref[number * 8 + chunk]
-            here = pl.multiple_of((2 * shard + core) * SHARD, SHARD)
-            values = ints_ref[pl.ds(here, SHARD), :]
-            row = start + here + lax.broadcasted_iota(jnp.int32, values.shape, 0)
-            keep = (row >= low) & (row < high)
-            parts.append(jnp.where(keep, values, jnp.zeros_like(values)))
-        for stage, numbers in enumerate(STAGES):
-            if number in numbers:
-                out_refs[stage][number - numbers[0]] = jnp.concatenate(parts, axis=0).T
+    for stage, numbers in enumerate(STAGES):
+        for at, number in enumerate(numbers):
+            parts = []
+            for chunk in range(8):
+                shard = place_ref[number * 8 + chunk]
+                values = held_ref[shard]
+                row = start + (2 * shard + core) * SHARD + lax.broadcasted_iota(jnp.int32, values.shape, 0)
+                keep = (row >= low) & (row < high)
+                parts.append(jnp.where(keep, values, jnp.zeros_like(values)))
+            out_refs[stage][at] = jnp.concatenate(parts, axis=0).T
 
 
 def prepare(place, ints, low, high):
@@ -132,12 +161,13 @@
     return pl.pallas_call(
         prepare_kernel,
         out_shape=[jax.ShapeDtypeStruct((len(numbers), COLS, 512), jnp.bfloat16) for numbers in STAGES],
-        in_specs=[pl.BlockSpec(memory_space=pltpu.SMEM)] + [vmem] * 3,
+        in_specs=[pl.BlockSpec(memory_space=pltpu.SMEM), pl.BlockSpec(memory_space=pltpu.HBM), vmem, vmem],
         out_specs=[vmem] * len(STAGES),
-        compiler_params=pltpu.CompilerParams(vmem_limit_bytes=VMEM_LIMIT),
-        cost_estimate=pl.CostEstimate(flops=0, bytes_accessed=12 << 20, transcendentals=0),
+        scratch_shapes=[pltpu.VMEM((64, SHARD, COLS), jnp.bfloat16), pltpu.SemaphoreType.DMA(())],
+        compiler_params=pltpu.CompilerParams(vmem_limit_bytes=VMEM_LIMIT),
+        cost_estimate=pl.CostEstimate(flops=0, bytes_accessed=6 << 20, transcendentals=0),
         name="prepare",
-    )(place, ints, low, high)
+    )(place, pltpu.with_memory_space_constraint(ints, pltpu.HBM), low, high)
 
 
 def early_kernel(count, fresh, near_ref, far_ref, *refs):
@@ -234,13 +264,19 @@
     permute = functools.partial(lax.ppermute, axis_name="blk")
 
     amp = jnp.transpose(amplitudes[:, 0, :])
-    copies = select(amp, pair_subset[None, :])
+    shard, copies = select(amp, pair_subset[None, :])
+    other_shard = permute(shard, perm=across())
+    exchange = functools.partial(
+        lax.all_to_all, axis_name="blk", split_axis=0, concat_axis=0, axis_index_groups=groups(), tiled=True
+    )
+    own = exchange(copies)
     pair_irrep, ints, copies = lax.optimization_barrier((pair_irrep, ladder_ints, copies))
     got = permute(ints, perm=across_core())
+
     t = jnp.arange(8, dtype=jnp.int32)
-    z_from = [z, z - 1, z + 1, z - 2, z + 2, z - 3, z + 3, z + 4]
+    z_from = [z, z - 1, z + 1, z - 2, z + 2, z + 4, z + 3, z - 3]
     zeros = [(t // 4 * Z + zz % Z) * X + t % 4 for zz in z_from]
-    hx_from = [(h, x), (h, x - 1), (h, x + 1), (h, x - 2), (h + 1, x), (h + 1, x - 1), (h + 1, x + 1), (h + 1, x + 2)]
+    hx_from = [(h, x), (h, x - 1), (h, x + 1), (h, x - 2), (h + 1, x + 2), (h + 1, x), (h + 1, x - 1), (h + 1, x + 1)]
     ones = [(hh % H * Z + t) * X + xx % X for hh, xx in hx_from]
     shards = jnp.where(c == 0, jnp.concatenate(zeros), jnp.concatenate(ones))
     place = jnp.concatenate([shards, c[None], (me * QUARTER)[None]]).astype(jnp.int32)
@@ -255,28 +291,23 @@
     high = jnp.sum(jnp.where(is_label, counts[1:, None], 0), axis=0)[None, :]
 
     own = lax.all_to_all(copies, "blk", 0, 0, axis_index_groups=groups(), tiled=True)
-    near = prepare(place, ladder_ints, low[:, :COLS], high[:, :COLS])
-    own, near = lax.optimization_barrier((own, near))
-    plus, minus = ring(1), ring(-1)
-    p1 = permute(own, perm=plus)
-    m1 = permute(own, perm=minus)
-    across = permute(own, perm=across_h())
-    far = prepare(place, got, low[:, COLS:], high[:, COLS:])
-    p2 = permute(p1, perm=plus)
-    m2 = permute(m1, perm=ring(-1, (0,)))
+    near = prepare(place, ladder_ints.reshape(64, 2, SHARD, COLS), low[:, :COLS], high[:, :COLS])
+    other_shard, near = lax.optimization_barrier((other_shard, near))
+    opposite = exchange(spread(other_shard))
+    p1 = permute(own, perm=ring(1))
+    m1 = permute(own, perm=ring(-1))
+    p2 = permute(p1, perm=ring(1))
+    m2 = permute(pick(c[None], m1, opposite), perm=ring(-1, (0,)) + ring(2, (1,)))
+    p3 = permute(opposite, perm=ring(1))
+    m3 = permute(opposite, perm=ring(-1))
+    far = prepare(place, got.reshape(64, 2, SHARD, COLS), low[:, COLS:], high[:, COLS:])
     so_far = early(near[0], far[0], (own, p1, m1))
-    p3_from = pick(c[None], p2, across)
-    m3_from = pick(c[None], m2, across)
-    p3 = permute(p3_from, perm=plus)
-    p3, so_far = lax.optimization_barrier((p3, so_far))
-    m3 = permute(m3_from, perm=minus)
-    so_far = early(near[1], far[1], (p2, m3_from), so_far)
-    p4 = permute(p3, perm=plus)
+    so_far = early(near[1], far[1], (p2, opposite), so_far)
     so_far = early(near[2], far[2], (p3, m3), so_far)
     own_subset = lax.dynamic_slice_in_dim(pair_subset, me * OWN, OWN, 0)
     gaps = jnp.take(occ_gap, own_subset)
     so_far, gaps = lax.optimization_barrier((so_far, gaps))
-    mine, away = tail(near[3], far[3], p4, so_far)
+    mine, away = tail(near[3], far[3], m2, so_far)
     other = permute(away, perm=across_core())
     dealt = deal(me[None], mine, other)
     terms = [dealt[0]]

time: 108 us -> 103 us (0.954); the launches traced: 107 us -> 101 us
  local copies, waits for them, and re-layouts: 10.1 us -> 3 us
  Pallas kernels: 13.1 us -> 16.2 us
  starting transfers between devices: 56.8 us -> 55.2 us
  waiting for transfers between devices: 25.9 us -> 24.5 us
    unnamed x42 -> x18, local copies, waits for them, and re-layouts: 8.72 us -> 0.83 us
    all_to_all x0 -> x1, waiting for transfers between devices: none -> 7.78 us  [body(): opposite = exchange(spread(other_shard))]
    ppermute x8 -> x7, waiting for transfers between devices: 11.8 us -> 4.81 us  [the longest x1 4.79 us: body(): p2 = permute(p1, perm=ring(1))]
    ppermute x1, starting transfers between devices: 8.4 us -> 1.92 us  [body(): other = permute(away, perm=across_core())]
    all_to_all x1, starting transfers between devices: 4.67 us -> 10 us  [body(): lax.all_to_all(copies, 'blk', 0, 0, axis_index_groups=groups(), tiled=True)]
    ppermute x8 -> x7, starting transfers between devices: 25 us -> 21 us  [the longest x1 3.97 us: body(): permute(pick(c[None], m1, opposite), perm=ring(-1, (0,)) + ring(2, (1,)))]
    all_to_all x0 -> x1, starting transfers between devices: none -> 3.49 us  [body(): opposite = exchange(spread(other_shard))]
    ppermute x3, waiting for transfers between devices: 7.44 us -> 4.96 us  [body(): lax.ppermute(dealt[step], 'grp', [(i, i ^ step) for i in range(GRP)])]
  transfers between devices with their start and end apart: 14 -> 14, of which waited for: 6 -> 7; matrix products, arithmetic and copies ran while one was open for 2% -> 4% of each run, Pallas kernels for 10% -> 13%
where the time goes in v3:
time: 103 us; the launch traced here: 101 us
  starting transfers between devices  55.2 us (54%)
  waiting for transfers between devices  24.5 us (24%)
  Pallas kernels  16.2 us (16%)
  local copies, waits for them, and re-layouts  3 us (3%)
  other arithmetic  1.7 us (2%)
    all_to_all x1, starting transfers between devices, body(): lax.all_to_all(copies, 'blk', 0, 0, axis_index_groups=groups(), tiled=True)  10 us
    ppermute x3, starting transfers between devices, body(): lax.ppermute(dealt[step], 'grp', [(i, i ^ step) for i in range(GRP)])  10 us
    ppermute x1, starting transfers between devices, body(): got = permute(ints, perm=across_core())  8.79 us
    all_to_all x1, waiting for transfers between devices, body(): opposite = exchange(spread(other_shard))  7.78 us
    pallas_call x2, Pallas kernels, prepare(): pl.pallas_call(prepare_kernel, out_shape=[jax.ShapeDtypeStruct((len(numbe...  6.08 us
    pallas_call x3, Pallas kernels, early(): pl.pallas_call(functools.partial(early_kernel, len(pieces), before is Non...  5.83 us
    all_to_all x1, waiting for transfers between devices, body(): lax.all_to_all(copies, 'blk', 0, 0, axis_index_groups=groups(), tiled=True)  5.04 us
    ppermute x3, waiting for transfers between devices, body(): lax.ppermute(dealt[step], 'grp', [(i, i ^ step) for i in range(GRP)])  4.96 us
  transfers between devices with their start and end apart: 14, of which 7 were waited for; matrix products, arithmetic and copies ran while one was open for 4% of the time, Pallas kernels for 13%

profile of v3, /device:TPU:1, one launch (start us, length us, event | category | flops | bytes accessed | tf_op | source)
XLA Modules:
  0.0 100.9 jit_solution(7987693224929872429)
XLA Ops:
  0.0 0.0 copy-start
  0.0 2.1 %select.55 = (bf16[64,512]{1,0:T(8,128)(2,1)S(1)}, bf16[512,512]{1,0:T(8,128)(2,1)}) custom-call(bf16[64,1024]{1,0:T(8,128)(2,1)} %bitcast.26, s32[1,512]{1,0:T(1,128)} %bitcast.29), custom_call_target="tpu_custom_call" | custom-call | tf_op jit(solution)/shard_map/select/pallas_call | solution.py:73
  2.1 8.8 %collective-permute-start.1 = (bf16[8192,256]{1,0:T(8,128)(2,1)}, bf16[8192,256]{1,0:T(8,128)(2,1)}, u32[]{:S(2)}, u32[]{:S(2)}) collective-permute-start(bf16[8192,256]{1,0:T(8,128)(2,1)} %param.7), channel_id=1, source_target_pairs={{0,4},{4,0},{8,12},{12,8},{16,20},{20,16},{24,28},{28,24},{32,36},... | collective-permute-start | bytes 12582920 | tf_op jit(solution)/shard_map/ppermute | solution.py:274
  10.9 2.1 %collective-permute-start = (bf16[64,512]{1,0:T(8,128)(2,1)S(1)}, bf16[64,512]{1,0:T(8,128)(2,1)S(1)}, u32[]{:S(2)}, u32[]{:S(2)}) collective-permute-start(bf16[64,512]{1,0:T(8,128)(2,1)S(1)} %get-tuple-element.31), channel_id=1, source_target_pairs={{0,128},{4,260},{8,136},{12,268},{16,144},{20,276},{24,152},{28,28... | collective-permute-start | bytes 196616 | tf_op jit(solution)/shard_map/ppermute | solution.py:268
  13.0 10.0 %all-to-all-start = ((bf16[8,64,512]{2,1,0:T(8,128)(2,1)}), bf16[8,64,512]{2,1,0:T(8,128)(2,1)S(1)}, u32[]{:S(2)}, u32[]{:S(2)}) async-start(bf16[8,64,512]{2,1,0:T(8,128)(2,1)} %bitcast.10), calls=%async_computation | async-start | bytes 1048576 | tf_op jit(solution)/shard_map/all_to_all | solution.py:293
  23.1 0.8 fusion.1
  24.0 1.3 %convert_reduce_fusion = s32[9]{0:T(128)S(1)} fusion(s32[32768]{0:T(1024)} %param.8), kind=kLoop, calls=%fused_computation.1 | loop fusion | flops 884727 | bytes 131108 | tf_op jit(solution)/shard_map/reduce_sum | solution.py:284
  25.3 0.1 concatenate.13
  25.4 0.1 concatenate.12
  25.5 0.1 fusion.4
  25.5 0.1 select_reduce_fusion
  25.7 0.1 pad_add_fusion.1.place_ref
  25.7 3.0 %prepare.2 = (bf16[3,256,512]{2,1,0:T(8,128)(2,1)S(1)}, bf16[2,256,512]{2,1,0:T(8,128)(2,1)S(1)}, bf16[2,256,512]{2,1,0:T(8,128)(2,1)S(1)}, bf16[1,256,512]{2,1,0:T(8,128)(2,1)S(1)}) custom-call(s32[66]{0:T(128)S(1)} %pad_add_fusion.1.place_ref, bf16[64,2,64,256]{3,2,1,0:T(8,128)(2,1)} %bitcast.25, s32[1,256]{1,0:T(1,128)S(1)} %get-tuple-element.83.low_ref, ...), custom_call_target="tpu_custom_call" | custom-call | bytes 6291456 | tf_op jit(solution)/shard_map/prepare/pallas_call | solution.py:161
  28.8 0.0 copy-start.1
  28.8 0.8 copy-done.1
  29.6 0.0 copy-start.3
  29.6 0.0 collective-permute-done.shard_ref
  29.6 0.8 spread.1
  30.4 5.0 %all-to-all-done = bf16[8,64,512]{2,1,0:T(8,128)(2,1)S(1)} async-done(((bf16[8,64,512]{2,1,0:T(8,128)(2,1)}), bf16[8,64,512]{2,1,0:T(8,128)(2,1)S(1)}, u32[]{:S(2)}, u32[]{:S(2)}) %all-to-all-start) | async-done | bytes 524320 | tf_op jit(solution)/shard_map/all_to_all | solution.py:293
  35.5 0.0 copy-done.3
  35.5 3.5 %all-to-all-start.1 = ((bf16[8,64,512]{2,1,0:T(8,128)(2,1)}), bf16[8,64,512]{2,1,0:T(8,128)(2,1)S(1)}, u32[]{:S(2)}, u32[]{:S(2)}) async-start(bf16[8,64,512]{2,1,0:T(8,128)(2,1)} %bitcast.12), calls=%async_computation.1 | async-start | bytes 1048576 | tf_op jit(solution)/shard_map/all_to_all | solution.py:296
  39.0 0.0 copy-done.5
  39.0 3.1 %collective-permute-start.6 = (bf16[512,512]{1,0:T(8,128)(2,1)S(1)}, bf16[512,512]{1,0:T(8,128)(2,1)}, u32[]{:S(2)}, u32[]{:S(2)}) collective-permute-start(bf16[512,512]{1,0:T(8,128)(2,1)S(1)} %bitcast.21), channel_id=1, source_target_pairs={{0,32},{4,12},{8,40},{12,20},{16,48},{20,28},{24,56},{28,4},{32,64... | collective-permute-start | bytes 1572872 | tf_op jit(solution)/shard_map/ppermute | solution.py:297
  42.1 3.4 %collective-permute-start.2 = (bf16[512,512]{1,0:T(8,128)(2,1)S(1)}, bf16[512,512]{1,0:T(8,128)(2,1)S(1)}, u32[]{:S(2)}, u32[]{:S(2)}) collective-permute-start(bf16[512,512]{1,0:T(8,128)(2,1)S(1)} %bitcast.22), channel_id=1, source_target_pairs={{0,224},{4,28},{8,232},{12,4},{16,240},{20,12},{24,248},{28,20},{3... | collective-permute-start | bytes 1572872 | tf_op jit(solution)/shard_map/ppermute | solution.py:298
  45.5 7.8 %all-to-all-done.1 = bf16[8,64,512]{2,1,0:T(8,128)(2,1)S(1)} async-done(((bf16[8,64,512]{2,1,0:T(8,128)(2,1)}), bf16[8,64,512]{2,1,0:T(8,128)(2,1)S(1)}, u32[]{:S(2)}, u32[]{:S(2)}) %all-to-all-start.1) | async-done | bytes 524320 | tf_op jit(solution)/shard_map/all_to_all | solution.py:296
  53.3 2.7 %collective-permute-start.4 = (bf16[512,512]{1,0:T(8,128)(2,1)S(1)}, bf16[512,512]{1,0:T(8,128)(2,1)}, u32[]{:S(2)}, u32[]{:S(2)}) collective-permute-start(bf16[512,512]{1,0:T(8,128)(2,1)S(1)} %bitcast.17), channel_id=1, source_target_pairs={{0,32},{4,12},{8,40},{12,20},{16,48},{20,28},{24,56},{28,4},{32,64... | collective-permute-start | bytes 1572872 | tf_op jit(solution)/shard_map/ppermute | solution.py:301
  56.0 3.8 %collective-permute-start.5 = (bf16[512,512]{1,0:T(8,128)(2,1)S(1)}, bf16[512,512]{1,0:T(8,128)(2,1)}, u32[]{:S(2)}, u32[]{:S(2)}) collective-permute-start(bf16[512,512]{1,0:T(8,128)(2,1)S(1)} %bitcast.18), channel_id=1, source_target_pairs={{0,224},{4,28},{8,232},{12,4},{16,240},{20,12},{24,248},{28,20},{3... | collective-permute-start | bytes 1572872 | tf_op jit(solution)/shard_map/ppermute | solution.py:302
  59.8 0.0 collective-permute-done.6.refs_1_
  59.8 1.9 %collective-permute-start.7 = (bf16[512,512]{1,0:T(8,128)(2,1)}, bf16[512,512]{1,0:T(8,128)(2,1)}, u32[]{:S(2)}, u32[]{:S(2)}) collective-permute-start(bf16[512,512]{1,0:T(8,128)(2,1)} %collective-permute-done.6.refs_1_), channel_id=1, source_target_pairs={{0,32},{4,12},{8,40},{12,20},{16,48},{20,28},{24,56},{28,4},{32,64... | collective-permute-start | bytes 1572872 | tf_op jit(solution)/shard_map/ppermute | solution.py:299
  61.7 0.0 collective-permute-done.2.first_ref.refs_2_
  61.8 4.0 %collective-permute-start.3 = (bf16[512,512]{1,0:T(8,128)(2,1)S(1)}, bf16[512,512]{1,0:T(8,128)(2,1)S(1)}, u32[]{:S(2)}, u32[]{:S(2)}) collective-permute-start(bf16[512,512]{1,0:T(8,128)(2,1)S(1)} %pick.1), channel_id=1, source_target_pairs={{0,224},{8,232},{16,240},{24,248},{32,0},{40,8},{48,16},{56,24},{6... | collective-permute-start | bytes 1572872 | tf_op jit(solution)/shard_map/ppermute | solution.py:300
  65.8 0.0 copy-done.8
  65.8 0.1 compare_select_fusion
  65.9 0.0 copy-done
  65.9 1.0 gather_fusion
  66.9 0.1 and_select_fusion
  67.0 0.0 collective-permute-done.1
  67.0 3.0 %prepare.3 = (bf16[3,256,512]{2,1,0:T(8,128)(2,1)S(1)}, bf16[2,256,512]{2,1,0:T(8,128)(2,1)S(1)}, bf16[2,256,512]{2,1,0:T(8,128)(2,1)S(1)}, bf16[1,256,512]{2,1,0:T(8,128)(2,1)S(1)}) custom-call(s32[66]{0:T(128)S(1)} %pad_add_fusion.1.place_ref, bf16[64,2,64,256]{3,2,1,0:T(8,128)(2,1)} %bitcast.9.ints_ref, s32[1,256]{1,0:T(1,128)S(1)} %get-tuple-element.84.low_ref, ...), custom_call_target="tpu_custom_call" | custom-call | bytes 6291456 | tf_op jit(solution)/shard_map/prepare/pallas_call | solution.py:161
  70.0 0.0 copy-start.4
  70.0 2.1 %early.3.refs_2_ = f32[512,512]{1,0:T(8,128)S(1)} custom-call(bf16[3,256,512]{2,1,0:T(8,128)(2,1)S(1)} %get-tuple-element.47.near_ref, bf16[3,256,512]{2,1,0:T(8,128)(2,1)S(1)} %get-tuple-element.48.far_ref, bf16[512,512]{1,0:T(8,128)(2,1)S(1)} %bitcast.23, bf16[512,512]{1,0:T(8,128)(2,1)} %collective-permute-done.6.refs_1_, ...), custom_call_target="tpu_custom_call" | custom-call | flops 805306368 | bytes 3145728 | tf_op jit(solution)/shard_map/early/pallas_call | solution.py:187
  72.1 4.8 %collective-permute-done.7.refs_0_ = bf16[512,512]{1,0:T(8,128)(2,1)} collective-permute-done((bf16[512,512]{1,0:T(8,128)(2,1)}, bf16[512,512]{1,0:T(8,128)(2,1)}, u32[]{:S(2)}, u32[]{:S(2)}) %collective-permute-start.7) | collective-permute-done | bytes 524320 | tf_op jit(solution)/shard_map/ppermute | solution.py:299
  76.9 0.0 copy-done.4
  76.9 1.8 %early.4.refs_2_ = f32[512,512]{1,0:T(8,128)S(1)} custom-call(bf16[2,256,512]{2,1,0:T(8,128)(2,1)S(1)} %copy-done.4, bf16[2,256,512]{2,1,0:T(8,128)(2,1)S(1)} %get-tuple-element.46.far_ref, bf16[512,512]{1,0:T(8,128)(2,1)} %collective-permute-done.7.refs_0_, bf16[512,512]{1,0:T(8,128)(2,1)S(1)} %bitcast.20, f32[512,512]{1,0:T(8,128)S(1)} %early.3.refs_2_), custom_call_target="tpu_custom_call" | custom-call | flops 536870912 | bytes 2097152 | tf_op jit(solution)/shard_map/early/pallas_call | solution.py:187
  78.7 0.0 collective-permute-done.4.refs_0_
  78.7 0.0 collective-permute-done.5.refs_1_
  78.7 0.0 copy-done.2
  78.7 0.0 copy-start.6
  78.7 1.9 %early.5.before_ref = f32[512,512]{1,0:T(8,128)S(1)} custom-call(bf16[2,256,512]{2,1,0:T(8,128)(2,1)S(1)} %copy-done.2, bf16[2,256,512]{2,1,0:T(8,128)(2,1)S(1)} %get-tuple-element.44.far_ref, bf16[512,512]{1,0:T(8,128)(2,1)} %collective-permute-done.4.refs_0_, bf16[512,512]{1,0:T(8,128)(2,1)} %collective-permute-done.5.refs_1_, f32[512,512]{1,0:T(8,128)S(1)} %early.4.refs_2_), custom_call_target="tpu_custom_call" | custom-call | flops 536870912 | bytes 2097152 | tf_op jit(solution)/shard_map/early/pallas_call | solution.py:187
  80.7 0.0 copy-start.7
  80.7 0.0 collective-permute-done.3.piece_ref
  80.7 0.0 copy-done.6
  80.7 0.4 tail.1
  81.2 1.9 %collective-permute-start.8 = (f32[4,256,128]{2,1,0:T(8,128)S(1)}, f32[4,256,128]{2,1,0:T(8,128)S(1)}, u32[]{:S(2)}, u32[]{:S(2)}) collective-permute-start(f32[4,256,128]{2,1,0:T(8,128)S(1)} %get-tuple-element.51), channel_id=1, source_target_pairs={{0,4},{4,0},{8,12},{12,8},{16,20},{20,16},{24,28},{28,24},{32,36},... | collective-permute-start | bytes 1572872 | tf_op jit(solution)/shard_map/ppermute | solution.py:311
  83.1 1.9 %collective-permute-done.8.other_ref = f32[4,256,128]{2,1,0:T(8,128)S(1)} collective-permute-done((f32[4,256,128]{2,1,0:T(8,128)S(1)}, f32[4,256,128]{2,1,0:T(8,128)S(1)}, u32[]{:S(2)}, u32[]{:S(2)}) %collective-permute-start.8) | collective-permute-done | bytes 524320 | tf_op jit(solution)/shard_map/ppermute | solution.py:311
  85.0 0.1 deal.1
  85.0 5.0 %collective-permute-start.10 = (f32[256,128]{1,0:T(8,128)S(1)}, f32[256,128]{1,0:T(8,128)S(1)}, u32[]{:S(2)}, u32[]{:S(2)}) collective-permute-start(f32[256,128]{1,0:T(8,128)S(1)} %get-tuple-element.54), channel_id=1, source_target_pairs={{0,2},{1,3},{2,0},{3,1},{4,6},{5,7},{6,4},{7,5},{8,10},{9,11},{10,... | collective-permute-start | bytes 393224 | tf_op jit(solution)/shard_map/ppermute | solution.py:315
  90.0 1.9 %collective-permute-start.11 = (f32[256,128]{1,0:T(8,128)S(1)}, f32[256,128]{1,0:T(8,128)S(1)}, u32[]{:S(2)}, u32[]{:S(2)}) collective-permute-start(f32[256,128]{1,0:T(8,128)S(1)} %get-tuple-element.55), channel_id=1, source_target_pairs={{0,1},{1,0},{2,3},{3,2},{4,5},{5,4},{6,7},{7,6},{8,9},{9,8},{10,11... | collective-permute-start | bytes 393224 | tf_op jit(solution)/shard_map/ppermute | solution.py:315
  92.0 3.1 %collective-permute-start.9 = (f32[256,128]{1,0:T(8,128)S(1)}, f32[256,128]{1,0:T(8,128)S(1)}, u32[]{:S(2)}, u32[]{:S(2)}) collective-permute-start(f32[256,128]{1,0:T(8,128)S(1)} %get-tuple-element.53), channel_id=1, source_target_pairs={{0,3},{1,2},{2,1},{3,0},{4,7},{5,6},{6,5},{7,4},{8,11},{9,10},{10,... | collective-permute-start | bytes 393224 | tf_op jit(solution)/shard_map/ppermute | solution.py:315
  95.1 0.1 copy.9.gap_ref
  95.2 1.2 %collective-permute-done.10.c_ref = f32[256,128]{1,0:T(8,128)S(1)} collective-permute-done((f32[256,128]{1,0:T(8,128)S(1)}, f32[256,128]{1,0:T(8,128)S(1)}, u32[]{:S(2)}, u32[]{:S(2)}) %collective-permute-start.10) | collective-permute-done | bytes 131104 | tf_op jit(solution)/shard_map/ppermute | solution.py:315
  96.4 2.1 %collective-permute-done.11.d_ref = f32[256,128]{1,0:T(8,128)S(1)} collective-permute-done((f32[256,128]{1,0:T(8,128)S(1)}, f32[256,128]{1,0:T(8,128)S(1)}, u32[]{:S(2)}, u32[]{:S(2)}) %collective-permute-start.11) | collective-permute-done | bytes 131104 | tf_op jit(solution)/shard_map/ppermute | solution.py:315
  98.5 1.7 %collective-permute-done.9.b_ref = f32[256,128]{1,0:T(8,128)S(1)} collective-permute-done((f32[256,128]{1,0:T(8,128)S(1)}, f32[256,128]{1,0:T(8,128)S(1)}, u32[]{:S(2)}, u32[]{:S(2)}) %collective-permute-start.9) | collective-permute-done | bytes 131104 | tf_op jit(solution)/shard_map/ppermute | solution.py:315
  100.1 0.0 copy-done.7
  100.1 0.8 close.1
  (16 shorter events, 0.1 us)
Async XLA Ops:
  0.0 65.9 %copy-start = (f32[1024]{0:T(1024)S(1)}, f32[1024]{0:T(1024)}, u32[]{:S(2)}) copy-start(f32[1024]{0:T(1024)} %param.9) | copy-start | bytes 12292
  2.1 64.8 %collective-permute-start.1 = (bf16[8192,256]{1,0:T(8,128)(2,1)}, bf16[8192,256]{1,0:T(8,128)(2,1)}, u32[]{:S(2)}, u32[]{:S(2)}) collective-permute-start(bf16[8192,256]{1,0:T(8,128)(2,1)} %param.7), channel_id=1, source_target_pairs={{0,4},{4,0},{8,12},{12,8},{16,20},{20,16},{24,28},{28,24},{32,36},... | collective-permute-start | bytes 12582920 | tf_op jit(solution)/shard_map/ppermute | solution.py:274
  10.9 18.7 %collective-permute-start = (bf16[64,512]{1,0:T(8,128)(2,1)S(1)}, bf16[64,512]{1,0:T(8,128)(2,1)S(1)}, u32[]{:S(2)}, u32[]{:S(2)}) collective-permute-start(bf16[64,512]{1,0:T(8,128)(2,1)S(1)} %get-tuple-element.31), channel_id=1, source_target_pairs={{0,128},{4,260},{8,136},{12,268},{16,144},{20,276},{24,152},{28,28... | collective-permute-start | bytes 196616 | tf_op jit(solution)/shard_map/ppermute | solution.py:268
  13.0 22.5 %all-to-all-start = ((bf16[8,64,512]{2,1,0:T(8,128)(2,1)}), bf16[8,64,512]{2,1,0:T(8,128)(2,1)S(1)}, u32[]{:S(2)}, u32[]{:S(2)}) async-start(bf16[8,64,512]{2,1,0:T(8,128)(2,1)} %bitcast.10), calls=%async_computation | async-start | bytes 1048576 | tf_op jit(solution)/shard_map/all_to_all | solution.py:293
  28.8 0.8 copy-start.1
  29.6 5.9 %copy-start.3 = (bf16[2,256,512]{2,1,0:T(8,128)(2,1)}, bf16[2,256,512]{2,1,0:T(8,128)(2,1)S(1)}, u32[]{:S(2)}) copy-start(bf16[2,256,512]{2,1,0:T(8,128)(2,1)S(1)} %get-tuple-element.45.near_ref) | copy-start | bytes 1572868
  29.6 9.4 %copy-start.5 = (bf16[1,256,512]{2,1,0:T(8,128)(2,1)}, bf16[1,256,512]{2,1,0:T(8,128)(2,1)S(1)}, u32[]{:S(2)}) copy-start(bf16[1,256,512]{2,1,0:T(8,128)(2,1)S(1)} %get-tuple-element.38.near_ref) | copy-start | bytes 786436
  29.6 36.2 %copy-start.8 = (s32[512]{0:T(512)S(1)}, s32[512]{0:T(512)}, u32[]{:S(2)}) copy-start(s32[512]{0:T(512)} %param.11) | copy-start | bytes 6148
  35.5 17.8 %all-to-all-start.1 = ((bf16[8,64,512]{2,1,0:T(8,128)(2,1)}), bf16[8,64,512]{2,1,0:T(8,128)(2,1)S(1)}, u32[]{:S(2)}, u32[]{:S(2)}) async-start(bf16[8,64,512]{2,1,0:T(8,128)(2,1)} %bitcast.12), calls=%async_computation.1 | async-start | bytes 1048576 | tf_op jit(solution)/shard_map/all_to_all | solution.py:296
  39.0 20.8 %collective-permute-start.6 = (bf16[512,512]{1,0:T(8,128)(2,1)S(1)}, bf16[512,512]{1,0:T(8,128)(2,1)}, u32[]{:S(2)}, u32[]{:S(2)}) collective-permute-start(bf16[512,512]{1,0:T(8,128)(2,1)S(1)} %bitcast.21), channel_id=1, source_target_pairs={{0,32},{4,12},{8,40},{12,20},{16,48},{20,28},{24,56},{28,4},{32,64... | collective-permute-start | bytes 1572872 | tf_op jit(solution)/shard_map/ppermute | solution.py:297
  42.1 19.6 %collective-permute-start.2 = (bf16[512,512]{1,0:T(8,128)(2,1)S(1)}, bf16[512,512]{1,0:T(8,128)(2,1)S(1)}, u32[]{:S(2)}, u32[]{:S(2)}) collective-permute-start(bf16[512,512]{1,0:T(8,128)(2,1)S(1)} %bitcast.22), channel_id=1, source_target_pairs={{0,224},{4,28},{8,232},{12,4},{16,240},{20,12},{24,248},{28,20},{3... | collective-permute-start | bytes 1572872 | tf_op jit(solution)/shard_map/ppermute | solution.py:298
  53.3 25.4 %collective-permute-start.4 = (bf16[512,512]{1,0:T(8,128)(2,1)S(1)}, bf16[512,512]{1,0:T(8,128)(2,1)}, u32[]{:S(2)}, u32[]{:S(2)}) collective-permute-start(bf16[512,512]{1,0:T(8,128)(2,1)S(1)} %bitcast.17), channel_id=1, source_target_pairs={{0,32},{4,12},{8,40},{12,20},{16,48},{20,28},{24,56},{28,4},{32,64... | collective-permute-start | bytes 1572872 | tf_op jit(solution)/shard_map/ppermute | solution.py:301
  56.0 22.7 %collective-permute-start.5 = (bf16[512,512]{1,0:T(8,128)(2,1)S(1)}, bf16[512,512]{1,0:T(8,128)(2,1)}, u32[]{:S(2)}, u32[]{:S(2)}) collective-permute-start(bf16[512,512]{1,0:T(8,128)(2,1)S(1)} %bitcast.18), channel_id=1, source_target_pairs={{0,224},{4,28},{8,232},{12,4},{16,240},{20,12},{24,248},{28,20},{3... | collective-permute-start | bytes 1572872 | tf_op jit(solution)/shard_map/ppermute | solution.py:302
  59.8 17.1 %collective-permute-start.7 = (bf16[512,512]{1,0:T(8,128)(2,1)}, bf16[512,512]{1,0:T(8,128)(2,1)}, u32[]{:S(2)}, u32[]{:S(2)}) collective-permute-start(bf16[512,512]{1,0:T(8,128)(2,1)} %collective-permute-done.6.refs_1_), channel_id=1, source_target_pairs={{0,32},{4,12},{8,40},{12,20},{16,48},{20,28},{24,56},{28,4},{32,64... | collective-permute-start | bytes 1572872 | tf_op jit(solution)/shard_map/ppermute | solution.py:299
  61.8 18.9 %collective-permute-start.3 = (bf16[512,512]{1,0:T(8,128)(2,1)S(1)}, bf16[512,512]{1,0:T(8,128)(2,1)S(1)}, u32[]{:S(2)}, u32[]{:S(2)}) collective-permute-start(bf16[512,512]{1,0:T(8,128)(2,1)S(1)} %pick.1), channel_id=1, source_target_pairs={{0,224},{8,232},{16,240},{24,248},{32,0},{40,8},{48,16},{56,24},{6... | collective-permute-start | bytes 1572872 | tf_op jit(solution)/shard_map/ppermute | solution.py:300
  70.0 6.9 %copy-start.4 = (bf16[2,256,512]{2,1,0:T(8,128)(2,1)S(1)}, bf16[2,256,512]{2,1,0:T(8,128)(2,1)}, u32[]{:S(2)}) copy-start(bf16[2,256,512]{2,1,0:T(8,128)(2,1)} %copy-done.3) | copy-start | bytes 1572868
  76.9 1.8 %copy-start.2 = (bf16[2,256,512]{2,1,0:T(8,128)(2,1)S(1)}, bf16[2,256,512]{2,1,0:T(8,128)(2,1)}, u32[]{:S(2)}) copy-start(bf16[2,256,512]{2,1,0:T(8,128)(2,1)} %copy-done.1) | copy-start | bytes 1572868
  78.7 2.0 %copy-start.6 = (bf16[1,256,512]{2,1,0:T(8,128)(2,1)S(1)}, bf16[1,256,512]{2,1,0:T(8,128)(2,1)}, u32[]{:S(2)}) copy-start(bf16[1,256,512]{2,1,0:T(8,128)(2,1)} %copy-done.5) | copy-start | bytes 786436
  80.7 19.4 %copy-start.7 = (f32[256]{0:T(256)S(1)}, f32[256]{0:T(256)}, u32[]{:S(2)}) copy-start(f32[256]{0:T(256)} %param.10) | copy-start | bytes 3076
  81.2 3.8 %collective-permute-start.8 = (f32[4,256,128]{2,1,0:T(8,128)S(1)}, f32[4,256,128]{2,1,0:T(8,128)S(1)}, u32[]{:S(2)}, u32[]{:S(2)}) collective-permute-start(f32[4,256,128]{2,1,0:T(8,128)S(1)} %get-tuple-element.51), channel_id=1, source_target_pairs={{0,4},{4,0},{8,12},{12,8},{16,20},{20,16},{24,28},{28,24},{32,36},... | collective-permute-start | bytes 1572872 | tf_op jit(solution)/shard_map/ppermute | solution.py:311
  85.0 11.4 %collective-permute-start.10 = (f32[256,128]{1,0:T(8,128)S(1)}, f32[256,128]{1,0:T(8,128)S(1)}, u32[]{:S(2)}, u32[]{:S(2)}) collective-permute-start(f32[256,128]{1,0:T(8,128)S(1)} %get-tuple-element.54), channel_id=1, source_target_pairs={{0,2},{1,3},{2,0},{3,1},{4,6},{5,7},{6,4},{7,5},{8,10},{9,11},{10,... | collective-permute-start | bytes 393224 | tf_op jit(solution)/shard_map/ppermute | solution.py:315
  90.0 8.4 %collective-permute-start.11 = (f32[256,128]{1,0:T(8,128)S(1)}, f32[256,128]{1,0:T(8,128)S(1)}, u32[]{:S(2)}, u32[]{:S(2)}) collective-permute-start(f32[256,128]{1,0:T(8,128)S(1)} %get-tuple-element.55), channel_id=1, source_target_pairs={{0,1},{1,0},{2,3},{3,2},{4,5},{5,4},{6,7},{7,6},{8,9},{9,8},{10,11... | collective-permute-start | bytes 393224 | tf_op jit(solution)/shard_map/ppermute | solution.py:315
  92.0 8.2 %collective-permute-start.9 = (f32[256,128]{1,0:T(8,128)S(1)}, f32[256,128]{1,0:T(8,128)S(1)}, u32[]{:S(2)}, u32[]{:S(2)}) collective-permute-start(f32[256,128]{1,0:T(8,128)S(1)} %get-tuple-element.53), channel_id=1, source_target_pairs={{0,3},{1,2},{2,1},{3,0},{4,7},{5,6},{6,5},{7,4},{8,11},{9,10},{10,... | collective-permute-start | bytes 393224 | tf_op jit(solution)/shard_map/ppermute | solution.py:315

commit v4 on v3

--- a/solution.py
+++ b/solution.py
@@ -15,7 +15,7 @@
 GRP = 4
 OWN = OCC // GRP
 VMEM_LIMIT = 12 * 1024 * 1024
-STAGES = ((0, 1, 2), (3, 5), (6, 7), (4,))
+STAGES = ((0, 1, 2), (3, 5), (7, 6), (4,))
 
 
 def index(h, z, x, c):
@@ -53,7 +53,7 @@
     return [(index(h, z, x, c), index(h, z, x, 1 - c)) for h, z, x, c in devices()]
 
 
-def select_kernel(amp_ref, subset_ref, out_ref, copies_ref, amp_here, subset_here, sems):
+def select_kernel(amp_ref, subset_ref, copies_ref, amp_here, subset_here, shard_ref, sems):
     fetch = [
         pltpu.make_async_copy(amp_ref, amp_here, sems.at[8]),
         pltpu.make_async_copy(subset_ref, subset_here, sems.at[9]),
@@ -64,33 +64,10 @@
         copy.wait()
     rows = amp_here.shape[1]
     hot = (lax.broadcasted_iota(jnp.int32, (rows, OCC), 0) == subset_here[...]).astype(jnp.bfloat16)
-    out_ref[...] = jnp.dot(amp_here[...], hot, preferred_element_type=jnp.float32).astype(jnp.bfloat16)
-    send_copies(out_ref, copies_ref, sems)
-
-
-def select(amplitudes, subset):
-    hbm, vmem = pl.BlockSpec(memory_space=pltpu.HBM), pl.BlockSpec(memory_space=pltpu.VMEM)
-    return pl.pallas_call(
-        select_kernel,
-        out_shape=[
-            jax.ShapeDtypeStruct((SHARD, OCC), jnp.bfloat16),
-            jax.ShapeDtypeStruct((8 * SHARD, OCC), jnp.bfloat16),
-        ],
-        in_specs=[hbm, hbm],
-        out_specs=[vmem, hbm],
-        scratch_shapes=[
-            pltpu.VMEM(amplitudes.shape, amplitudes.dtype),
-            pltpu.VMEM(subset.shape, subset.dtype),
-            pltpu.SemaphoreType.DMA((10,)),
-        ],
-        compiler_params=pltpu.CompilerParams(vmem_limit_bytes=VMEM_LIMIT),
-        name="select",
-    )(pltpu.with_memory_space_constraint(amplitudes, pltpu.HBM), pltpu.with_memory_space_constraint(subset, pltpu.HBM))
-
-
-def send_copies(shard_ref, out_ref, sems):
+    shard_ref[...] = jnp.dot(amp_here[...], hot, preferred_element_type=jnp.float32).astype(jnp.bfloat16)
     copies = [
-        pltpu.make_async_copy(shard_ref, out_ref.at[pl.ds(copy * SHARD, SHARD), :], sems.at[copy]) for copy in range(8)
+        pltpu.make_async_copy(shard_ref, copies_ref.at[pl.ds(copy * SHARD, SHARD), :], sems.at[copy])
+        for copy in range(8)
     ]
     for copy in copies:
         copy.start()
@@ -98,20 +75,22 @@
         copy.wait()
 
 
-def spread_kernel(shard_ref, out_ref, sems):
-    send_copies(shard_ref, out_ref, sems)
-
-
-def spread(shard):
-    return pl.pallas_call(
-        spread_kernel,
+def select(amplitudes, subset):
+    hbm = pl.BlockSpec(memory_space=pltpu.HBM)
+    return pl.pallas_call(
+        select_kernel,
         out_shape=jax.ShapeDtypeStruct((8 * SHARD, OCC), jnp.bfloat16),
-        in_specs=[pl.BlockSpec(memory_space=pltpu.VMEM)],
-        out_specs=pl.BlockSpec(memory_space=pltpu.HBM),
-        scratch_shapes=[pltpu.SemaphoreType.DMA((8,))],
-        compiler_params=pltpu.CompilerParams(vmem_limit_bytes=VMEM_LIMIT),
-        name="spread",
-    )(shard)
+        in_specs=[hbm, hbm],
+        out_specs=hbm,
+        scratch_shapes=[
+            pltpu.VMEM(amplitudes.shape, amplitudes.dtype),
+            pltpu.VMEM(subset.shape, subset.dtype),
+            pltpu.VMEM((SHARD, OCC), jnp.bfloat16),
+            pltpu.SemaphoreType.DMA((10,)),
+        ],
+        compiler_params=pltpu.CompilerParams(vmem_limit_bytes=VMEM_LIMIT),
+        name="select",
+    )(pltpu.with_memory_space_constraint(amplitudes, pltpu.HBM), pltpu.with_memory_space_constraint(subset, pltpu.HBM))
 
 
 def pick_kernel(core_ref, first_ref, second_ref, out_ref):
@@ -264,8 +243,7 @@
     permute = functools.partial(lax.ppermute, axis_name="blk")
 
     amp = jnp.transpose(amplitudes[:, 0, :])
-    shard, copies = select(amp, pair_subset[None, :])
-    other_shard = permute(shard, perm=across())
+    copies = select(amp, pair_subset[None, :])
     exchange = functools.partial(
         lax.all_to_all, axis_name="blk", split_axis=0, concat_axis=0, axis_index_groups=groups(), tiled=True
     )
@@ -292,21 +270,21 @@
 
     own = lax.all_to_all(copies, "blk", 0, 0, axis_index_groups=groups(), tiled=True)
     near = prepare(place, ladder_ints.reshape(64, 2, SHARD, COLS), low[:, :COLS], high[:, :COLS])
-    other_shard, near = lax.optimization_barrier((other_shard, near))
-    opposite = exchange(spread(other_shard))
+    own, near = lax.optimization_barrier((own, near))
+    opposite = permute(own, perm=across())
+    far = prepare(place, got.reshape(64, 2, SHARD, COLS), low[:, COLS:], high[:, COLS:])
+    own_subset = lax.dynamic_slice_in_dim(pair_subset, me * OWN, OWN, 0)
+    gaps = jnp.take(occ_gap, own_subset)
+    opposite, far, gaps = lax.optimization_barrier((opposite, far, gaps))
     p1 = permute(own, perm=ring(1))
     m1 = permute(own, perm=ring(-1))
     p2 = permute(p1, perm=ring(1))
     m2 = permute(pick(c[None], m1, opposite), perm=ring(-1, (0,)) + ring(2, (1,)))
+    m3 = permute(opposite, perm=ring(-1))
     p3 = permute(opposite, perm=ring(1))
-    m3 = permute(opposite, perm=ring(-1))
-    far = prepare(place, got.reshape(64, 2, SHARD, COLS), low[:, COLS:], high[:, COLS:])
     so_far = early(near[0], far[0], (own, p1, m1))
     so_far = early(near[1], far[1], (p2, opposite), so_far)
-    so_far = early(near[2], far[2], (p3, m3), so_far)
-    own_subset = lax.dynamic_slice_in_dim(pair_subset, me * OWN, OWN, 0)
-    gaps = jnp.take(occ_gap, own_subset)
-    so_far, gaps = lax.optimization_barrier((so_far, gaps))
+    so_far = early(near[2], far[2], (m3, p3), so_far)
     mine, away = tail(near[3], far[3], m2, so_far)
     other = permute(away, perm=across_core())
     dealt = deal(me[None], mine, other)

time: 103 us -> 96.1 us (0.933); the launches traced: 101 us -> 95.4 us
  Pallas kernels: 16.2 us -> 13 us
  waiting for transfers between devices: 24.5 us -> 23.3 us
    ppermute x1, waiting for transfers between devices: 0.01 us -> 9.14 us  [body(): p3 = permute(opposite, perm=ring(1))]
    all_to_all x1 -> x0, waiting for transfers between devices: 7.78 us -> none  [body(): opposite = exchange(spread(other_shard))]
    ppermute x1, starting transfers between devices: 2.08 us -> 7.45 us  [body(): opposite = permute(own, perm=across())]
    all_to_all x1, starting transfers between devices: 10 us -> 4.67 us  [body(): lax.all_to_all(copies, 'blk', 0, 0, axis_index_groups=groups(), tiled=True)]
    ppermute x1, waiting for transfers between devices: 4.79 us -> 0.01 us  [body(): p2 = permute(p1, perm=ring(1))]
    ppermute x1, starting transfers between devices: 1.92 us -> 6.11 us  [body(): other = permute(away, perm=across_core())]
    all_to_all x1 -> x0, starting transfers between devices: 3.49 us -> none  [body(): opposite = exchange(spread(other_shard))]
    pallas_call x3, Pallas kernels: 5.83 us -> 3.43 us  [early(): pl.pallas_call(functools.partial(early_kernel, len(pieces), before is Non...]
  transfers between devices with their start and end apart: 14 -> 13, of which waited for: 7 -> 5; matrix products, arithmetic and copies ran while one was open for 4% -> 2% of each run, Pallas kernels for 13% -> 10%
where the time goes in v4:
time: 96.1 us; the launch traced here: 95.4 us
  starting transfers between devices  56 us (58%)
  waiting for transfers between devices  23.3 us (24%)
  Pallas kernels  13 us (14%)
  local copies, waits for them, and re-layouts  2.12 us (2%)
    ppermute x3, starting transfers between devices, body(): lax.ppermute(dealt[step], 'grp', [(i, i ^ step) for i in range(GRP)])  10.9 us
    ppermute x1, waiting for transfers between devices, body(): p3 = permute(opposite, perm=ring(1))  9.14 us
    ppermute x1, starting transfers between devices, body(): got = permute(ints, perm=across_core())  8.79 us
    ppermute x1, starting transfers between devices, body(): opposite = permute(own, perm=across())  7.45 us
    all_to_all x1, waiting for transfers between devices, body(): lax.all_to_all(copies, 'blk', 0, 0, axis_index_groups=groups(), tiled=True)  7.39 us
    ppermute x1, starting transfers between devices, body(): other = permute(away, perm=across_core())  6.11 us
    pallas_call x2, Pallas kernels, prepare(): pl.pallas_call(prepare_kernel, out_shape=[jax.ShapeDtypeStruct((len(numbe...  6.08 us
    ppermute x3, waiting for transfers between devices, body(): lax.ppermute(dealt[step], 'grp', [(i, i ^ step) for i in range(GRP)])  5.21 us
  transfers between devices with their start and end apart: 13, of which 5 were waited for; matrix products, arithmetic and copies ran while one was open for 2% of the time, Pallas kernels for 10%

profile of v4, /device:TPU:1, one launch (start us, length us, event | category | flops | bytes accessed | tf_op | source)
XLA Modules:
  0.0 95.4 jit_solution(17621096879065715266)
XLA Ops:
  0.0 0.0 copy-start
  0.0 0.0 copy-start.4
  0.0 2.1 %select.55 = bf16[512,512]{1,0:T(8,128)(2,1)} custom-call(bf16[64,1024]{1,0:T(8,128)(2,1)} %bitcast.21, s32[1,512]{1,0:T(1,128)} %bitcast.24), custom_call_target="tpu_custom_call" | custom-call | tf_op jit(solution)/shard_map/select/pallas_call | solution.py:80
  2.1 8.8 %collective-permute-start.1 = (bf16[8192,256]{1,0:T(8,128)(2,1)}, bf16[8192,256]{1,0:T(8,128)(2,1)}, u32[]{:S(2)}, u32[]{:S(2)}) collective-permute-start(bf16[8192,256]{1,0:T(8,128)(2,1)} %param.7), channel_id=1, source_target_pairs={{0,4},{4,0},{8,12},{12,8},{16,20},{20,16},{24,28},{28,24},{32,36},... | collective-permute-start | bytes 12582920 | tf_op jit(solution)/shard_map/ppermute | solution.py:252
  10.9 4.7 %all-to-all-start = ((bf16[8,64,512]{2,1,0:T(8,128)(2,1)}), bf16[8,64,512]{2,1,0:T(8,128)(2,1)S(1)}, u32[]{:S(2)}, u32[]{:S(2)}) async-start(bf16[8,64,512]{2,1,0:T(8,128)(2,1)} %bitcast.4), calls=%async_computation | async-start | bytes 1048576 | tf_op jit(solution)/shard_map/all_to_all | solution.py:271
  15.7 0.1 concatenate.13
  15.8 0.1 concatenate.12
  15.9 0.0 copy-done.4
  15.9 0.1 fusion.1
  16.0 0.1 pad_add_fusion.1.place_ref
  16.0 0.4 convert_reduce_fusion
  16.4 0.1 fusion.4
  16.5 0.1 select_reduce_fusion
  16.6 0.0 copy-start.5
  16.6 3.0 %prepare.2 = (bf16[3,256,512]{2,1,0:T(8,128)(2,1)S(1)}, bf16[2,256,512]{2,1,0:T(8,128)(2,1)S(1)}, bf16[2,256,512]{2,1,0:T(8,128)(2,1)S(1)}, bf16[1,256,512]{2,1,0:T(8,128)(2,1)S(1)}) custom-call(s32[66]{0:T(128)S(1)} %pad_add_fusion.1.place_ref, bf16[64,2,64,256]{3,2,1,0:T(8,128)(2,1)} %bitcast.20, s32[1,256]{1,0:T(1,128)S(1)} %get-tuple-element.87.low_ref, ...), custom_call_target="tpu_custom_call" | custom-call | bytes 6291456 | tf_op jit(solution)/shard_map/prepare/pallas_call | solution.py:140
  19.7 0.0 copy-start.1
  19.7 0.7 copy-done.1
  20.4 7.4 %all-to-all-done = bf16[8,64,512]{2,1,0:T(8,128)(2,1)S(1)} async-done(((bf16[8,64,512]{2,1,0:T(8,128)(2,1)}), bf16[8,64,512]{2,1,0:T(8,128)(2,1)S(1)}, u32[]{:S(2)}, u32[]{:S(2)}) %all-to-all-start) | async-done | bytes 524320 | tf_op jit(solution)/shard_map/all_to_all | solution.py:271
  27.8 3.1 %collective-permute-start.6 = (bf16[512,512]{1,0:T(8,128)(2,1)S(1)}, bf16[512,512]{1,0:T(8,128)(2,1)}, u32[]{:S(2)}, u32[]{:S(2)}) collective-permute-start(bf16[512,512]{1,0:T(8,128)(2,1)S(1)} %bitcast.15), channel_id=1, source_target_pairs={{0,32},{4,12},{8,40},{12,20},{16,48},{20,28},{24,56},{28,4},{32,64... | collective-permute-start | bytes 1572872 | tf_op jit(solution)/shard_map/ppermute | solution.py:279
  30.9 7.5 %collective-permute-start = (bf16[512,512]{1,0:T(8,128)(2,1)S(1)}, bf16[512,512]{1,0:T(8,128)(2,1)S(1)}, u32[]{:S(2)}, u32[]{:S(2)}) collective-permute-start(bf16[512,512]{1,0:T(8,128)(2,1)S(1)} %bitcast.16), channel_id=1, source_target_pairs={{0,128},{4,260},{8,136},{12,268},{16,144},{20,276},{24,152},{28,28... | collective-permute-start | bytes 1572872 | tf_op jit(solution)/shard_map/ppermute | solution.py:274
  38.3 3.4 %collective-permute-start.2 = (bf16[512,512]{1,0:T(8,128)(2,1)S(1)}, bf16[512,512]{1,0:T(8,128)(2,1)S(1)}, u32[]{:S(2)}, u32[]{:S(2)}) collective-permute-start(bf16[512,512]{1,0:T(8,128)(2,1)S(1)} %bitcast.17), channel_id=1, source_target_pairs={{0,224},{4,28},{8,232},{12,4},{16,240},{20,12},{24,248},{28,20},{3... | collective-permute-start | bytes 1572872 | tf_op jit(solution)/shard_map/ppermute | solution.py:280
  41.7 0.0 copy-done.5
  41.7 0.1 compare_select_fusion
  41.8 0.0 copy-done
  41.8 1.0 %gather_fusion = f32[128]{0:T(128)S(1)} fusion(f32[1024]{0:T(1024)S(1)} %copy-done, s32[1024]{0:T(1024)S(1)} %pad_clamp_fusion), kind=kCustom, calls=%fused_computation | custom fusion | bytes 1536 | tf_op jit(solution)/shard_map/jit(_take)/gather | solution.py:277
  42.8 0.0 collective-permute-done.6.refs_1_
  42.8 1.9 %collective-permute-start.7 = (bf16[512,512]{1,0:T(8,128)(2,1)}, bf16[512,512]{1,0:T(8,128)(2,1)S(1)}, u32[]{:S(2)}, u32[]{:S(2)}) collective-permute-start(bf16[512,512]{1,0:T(8,128)(2,1)} %collective-permute-done.6.refs_1_), channel_id=1, source_target_pairs={{0,32},{4,12},{8,40},{12,20},{16,48},{20,28},{24,56},{28,4},{32,64... | collective-permute-start | bytes 1572872 | tf_op jit(solution)/shard_map/ppermute | solution.py:281
  44.7 0.1 and_select_fusion
  44.8 0.0 collective-permute-done.1
  44.8 3.0 %prepare.3 = (bf16[3,256,512]{2,1,0:T(8,128)(2,1)S(1)}, bf16[2,256,512]{2,1,0:T(8,128)(2,1)S(1)}, bf16[2,256,512]{2,1,0:T(8,128)(2,1)S(1)}, bf16[1,256,512]{2,1,0:T(8,128)(2,1)S(1)}) custom-call(s32[66]{0:T(128)S(1)} %pad_add_fusion.1.place_ref, bf16[64,2,64,256]{3,2,1,0:T(8,128)(2,1)} %bitcast.11.ints_ref, s32[1,256]{1,0:T(1,128)S(1)} %get-tuple-element.88.low_ref, ...), custom_call_target="tpu_custom_call" | custom-call | bytes 6291456 | tf_op jit(solution)/shard_map/prepare/pallas_call | solution.py:140
  47.9 0.0 collective-permute-done.second_ref.refs_1_
  47.9 4.6 %collective-permute-start.4 = (bf16[512,512]{1,0:T(8,128)(2,1)S(1)}, bf16[512,512]{1,0:T(8,128)(2,1)S(1)}, u32[]{:S(2)}, u32[]{:S(2)}) collective-permute-start(bf16[512,512]{1,0:T(8,128)(2,1)S(1)} %collective-permute-done.second_ref.refs_1_), channel_id=1, source_target_pairs={{0,224},{4,28},{8,232},{12,4},{16,240},{20,12},{24,248},{28,20},{3... | collective-permute-start | bytes 1572872 | tf_op jit(solution)/shard_map/ppermute | solution.py:283
  52.5 1.9 %collective-permute-start.5 = (bf16[512,512]{1,0:T(8,128)(2,1)S(1)}, bf16[512,512]{1,0:T(8,128)(2,1)S(1)}, u32[]{:S(2)}, u32[]{:S(2)}) collective-permute-start(bf16[512,512]{1,0:T(8,128)(2,1)S(1)} %collective-permute-done.second_ref.refs_1_), channel_id=1, source_target_pairs={{0,32},{4,12},{8,40},{12,20},{16,48},{20,28},{24,56},{28,4},{32,64... | collective-permute-start | bytes 1572872 | tf_op jit(solution)/shard_map/ppermute | solution.py:284
  54.4 0.0 collective-permute-done.2.first_ref.refs_2_
  54.5 3.1 %collective-permute-start.3 = (bf16[512,512]{1,0:T(8,128)(2,1)S(1)}, bf16[512,512]{1,0:T(8,128)(2,1)S(1)}, u32[]{:S(2)}, u32[]{:S(2)}) collective-permute-start(bf16[512,512]{1,0:T(8,128)(2,1)S(1)} %pick.1), channel_id=1, source_target_pairs={{0,224},{8,232},{16,240},{24,248},{32,0},{40,8},{48,16},{56,24},{6... | collective-permute-start | bytes 1572872 | tf_op jit(solution)/shard_map/ppermute | solution.py:282
  57.6 2.0 %early.3.refs_2_ = f32[512,512]{1,0:T(8,128)S(1)} custom-call(bf16[3,256,512]{2,1,0:T(8,128)(2,1)S(1)} %get-tuple-element.52.near_ref, bf16[3,256,512]{2,1,0:T(8,128)(2,1)S(1)} %get-tuple-element.53.far_ref, bf16[512,512]{1,0:T(8,128)(2,1)S(1)} %bitcast.18, bf16[512,512]{1,0:T(8,128)(2,1)} %collective-permute-done.6.refs_1_, ...), custom_call_target="tpu_custom_call" | custom-call | flops 805306368 | bytes 3145728 | tf_op jit(solution)/shard_map/early/pallas_call | solution.py:166
  59.6 0.0 collective-permute-done.7.refs_0_
  59.6 0.7 early.4.refs_2_
  60.4 0.0 copy-start.2
  60.4 0.0 collective-permute-done.4.refs_0_
  60.4 9.1 %collective-permute-done.5.refs_1_ = bf16[512,512]{1,0:T(8,128)(2,1)S(1)} collective-permute-done((bf16[512,512]{1,0:T(8,128)(2,1)S(1)}, bf16[512,512]{1,0:T(8,128)(2,1)S(1)}, u32[]{:S(2)}, u32[]{:S(2)}) %collective-permute-start.5) | collective-permute-done | bytes 524320 | tf_op jit(solution)/shard_map/ppermute | solution.py:284
  69.5 0.7 early.5.before_ref
  70.2 0.0 copy-start.3
  70.2 0.0 collective-permute-done.3.piece_ref
  70.2 0.0 copy-done.2
  70.3 0.4 tail.1
  70.7 6.1 %collective-permute-start.8 = (f32[4,256,128]{2,1,0:T(8,128)S(1)}, f32[4,256,128]{2,1,0:T(8,128)S(1)}, u32[]{:S(2)}, u32[]{:S(2)}) collective-permute-start(f32[4,256,128]{2,1,0:T(8,128)S(1)} %get-tuple-element.55), channel_id=1, source_target_pairs={{0,4},{4,0},{8,12},{12,8},{16,20},{20,16},{24,28},{28,24},{32,36},... | collective-permute-start | bytes 1572872 | tf_op jit(solution)/shard_map/ppermute | solution.py:289
  76.8 1.5 %collective-permute-done.8.other_ref = f32[4,256,128]{2,1,0:T(8,128)S(1)} collective-permute-done((f32[4,256,128]{2,1,0:T(8,128)S(1)}, f32[4,256,128]{2,1,0:T(8,128)S(1)}, u32[]{:S(2)}, u32[]{:S(2)}) %collective-permute-start.8) | collective-permute-done | bytes 524320 | tf_op jit(solution)/shard_map/ppermute | solution.py:289
  78.3 0.1 deal.1
  78.4 4.8 %collective-permute-start.10 = (f32[256,128]{1,0:T(8,128)S(1)}, f32[256,128]{1,0:T(8,128)S(1)}, u32[]{:S(2)}, u32[]{:S(2)}) collective-permute-start(f32[256,128]{1,0:T(8,128)S(1)} %get-tuple-element.58), channel_id=1, source_target_pairs={{0,2},{1,3},{2,0},{3,1},{4,6},{5,7},{6,4},{7,5},{8,10},{9,11},{10,... | collective-permute-start | bytes 393224 | tf_op jit(solution)/shard_map/ppermute | solution.py:293
  83.2 2.1 %collective-permute-start.11 = (f32[256,128]{1,0:T(8,128)S(1)}, f32[256,128]{1,0:T(8,128)S(1)}, u32[]{:S(2)}, u32[]{:S(2)}) collective-permute-start(f32[256,128]{1,0:T(8,128)S(1)} %get-tuple-element.59), channel_id=1, source_target_pairs={{0,1},{1,0},{2,3},{3,2},{4,5},{5,4},{6,7},{7,6},{8,9},{9,8},{10,11... | collective-permute-start | bytes 393224 | tf_op jit(solution)/shard_map/ppermute | solution.py:293
  85.3 4.0 %collective-permute-start.9 = (f32[256,128]{1,0:T(8,128)S(1)}, f32[256,128]{1,0:T(8,128)S(1)}, u32[]{:S(2)}, u32[]{:S(2)}) collective-permute-start(f32[256,128]{1,0:T(8,128)S(1)} %get-tuple-element.57), channel_id=1, source_target_pairs={{0,3},{1,2},{2,1},{3,0},{4,7},{5,6},{6,5},{7,4},{8,11},{9,10},{10,... | collective-permute-start | bytes 393224 | tf_op jit(solution)/shard_map/ppermute | solution.py:293
  89.3 0.1 copy.9.gap_ref
  89.4 0.0 collective-permute-done.10.c_ref
  89.5 0.5 collective-permute-done.11.d_ref
  89.9 4.7 %collective-permute-done.9.b_ref = f32[256,128]{1,0:T(8,128)S(1)} collective-permute-done((f32[256,128]{1,0:T(8,128)S(1)}, f32[256,128]{1,0:T(8,128)S(1)}, u32[]{:S(2)}, u32[]{:S(2)}) %collective-permute-start.9) | collective-permute-done | bytes 131104 | tf_op jit(solution)/shard_map/ppermute | solution.py:293
  94.7 0.0 copy-done.3
  94.7 0.8 close.1
  (13 shorter events, 0.1 us)
Async XLA Ops:
  0.0 41.8 %copy-start = (f32[1024]{0:T(1024)S(1)}, f32[1024]{0:T(1024)}, u32[]{:S(2)}) copy-start(f32[1024]{0:T(1024)} %param.9) | copy-start | bytes 12292
  0.0 15.9 %copy-start.4 = (s32[32768]{0:T(1024)S(1)}, s32[32768]{0:T(1024)}, u32[]{:S(2)}) copy-start(s32[32768]{0:T(1024)} %param.8) | copy-start | bytes 393220
  2.1 42.7 %collective-permute-start.1 = (bf16[8192,256]{1,0:T(8,128)(2,1)}, bf16[8192,256]{1,0:T(8,128)(2,1)}, u32[]{:S(2)}, u32[]{:S(2)}) collective-permute-start(bf16[8192,256]{1,0:T(8,128)(2,1)} %param.7), channel_id=1, source_target_pairs={{0,4},{4,0},{8,12},{12,8},{16,20},{20,16},{24,28},{28,24},{32,36},... | collective-permute-start | bytes 12582920 | tf_op jit(solution)/shard_map/ppermute | solution.py:252
  10.9 16.8 %all-to-all-start = ((bf16[8,64,512]{2,1,0:T(8,128)(2,1)}), bf16[8,64,512]{2,1,0:T(8,128)(2,1)S(1)}, u32[]{:S(2)}, u32[]{:S(2)}) async-start(bf16[8,64,512]{2,1,0:T(8,128)(2,1)} %bitcast.4), calls=%async_computation | async-start | bytes 1048576 | tf_op jit(solution)/shard_map/all_to_all | solution.py:271
  16.6 25.1 %copy-start.5 = (s32[512]{0:T(512)S(1)}, s32[512]{0:T(512)}, u32[]{:S(2)}) copy-start(s32[512]{0:T(512)} %param.11) | copy-start | bytes 6148
  19.7 0.7 copy-start.1
  27.8 15.0 %collective-permute-start.6 = (bf16[512,512]{1,0:T(8,128)(2,1)S(1)}, bf16[512,512]{1,0:T(8,128)(2,1)}, u32[]{:S(2)}, u32[]{:S(2)}) collective-permute-start(bf16[512,512]{1,0:T(8,128)(2,1)S(1)} %bitcast.15), channel_id=1, source_target_pairs={{0,32},{4,12},{8,40},{12,20},{16,48},{20,28},{24,56},{28,4},{32,64... | collective-permute-start | bytes 1572872 | tf_op jit(solution)/shard_map/ppermute | solution.py:279
  30.9 17.0 %collective-permute-start = (bf16[512,512]{1,0:T(8,128)(2,1)S(1)}, bf16[512,512]{1,0:T(8,128)(2,1)S(1)}, u32[]{:S(2)}, u32[]{:S(2)}) collective-permute-start(bf16[512,512]{1,0:T(8,128)(2,1)S(1)} %bitcast.16), channel_id=1, source_target_pairs={{0,128},{4,260},{8,136},{12,268},{16,144},{20,276},{24,152},{28,28... | collective-permute-start | bytes 1572872 | tf_op jit(solution)/shard_map/ppermute | solution.py:274
  38.3 16.1 %collective-permute-start.2 = (bf16[512,512]{1,0:T(8,128)(2,1)S(1)}, bf16[512,512]{1,0:T(8,128)(2,1)S(1)}, u32[]{:S(2)}, u32[]{:S(2)}) collective-permute-start(bf16[512,512]{1,0:T(8,128)(2,1)S(1)} %bitcast.17), channel_id=1, source_target_pairs={{0,224},{4,28},{8,232},{12,4},{16,240},{20,12},{24,248},{28,20},{3... | collective-permute-start | bytes 1572872 | tf_op jit(solution)/shard_map/ppermute | solution.py:280
  42.8 16.8 %collective-permute-start.7 = (bf16[512,512]{1,0:T(8,128)(2,1)}, bf16[512,512]{1,0:T(8,128)(2,1)S(1)}, u32[]{:S(2)}, u32[]{:S(2)}) collective-permute-start(bf16[512,512]{1,0:T(8,128)(2,1)} %collective-permute-done.6.refs_1_), channel_id=1, source_target_pairs={{0,32},{4,12},{8,40},{12,20},{16,48},{20,28},{24,56},{28,4},{32,64... | collective-permute-start | bytes 1572872 | tf_op jit(solution)/shard_map/ppermute | solution.py:281
  47.9 12.5 %collective-permute-start.4 = (bf16[512,512]{1,0:T(8,128)(2,1)S(1)}, bf16[512,512]{1,0:T(8,128)(2,1)S(1)}, u32[]{:S(2)}, u32[]{:S(2)}) collective-permute-start(bf16[512,512]{1,0:T(8,128)(2,1)S(1)} %collective-permute-done.second_ref.refs_1_), channel_id=1, source_target_pairs={{0,224},{4,28},{8,232},{12,4},{16,240},{20,12},{24,248},{28,20},{3... | collective-permute-start | bytes 1572872 | tf_op jit(solution)/shard_map/ppermute | solution.py:283
  52.5 17.0 %collective-permute-start.5 = (bf16[512,512]{1,0:T(8,128)(2,1)S(1)}, bf16[512,512]{1,0:T(8,128)(2,1)S(1)}, u32[]{:S(2)}, u32[]{:S(2)}) collective-permute-start(bf16[512,512]{1,0:T(8,128)(2,1)S(1)} %collective-permute-done.second_ref.refs_1_), channel_id=1, source_target_pairs={{0,32},{4,12},{8,40},{12,20},{16,48},{20,28},{24,56},{28,4},{32,64... | collective-permute-start | bytes 1572872 | tf_op jit(solution)/shard_map/ppermute | solution.py:284
  54.5 15.8 %collective-permute-start.3 = (bf16[512,512]{1,0:T(8,128)(2,1)S(1)}, bf16[512,512]{1,0:T(8,128)(2,1)S(1)}, u32[]{:S(2)}, u32[]{:S(2)}) collective-permute-start(bf16[512,512]{1,0:T(8,128)(2,1)S(1)} %pick.1), channel_id=1, source_target_pairs={{0,224},{8,232},{16,240},{24,248},{32,0},{40,8},{48,16},{56,24},{6... | collective-permute-start | bytes 1572872 | tf_op jit(solution)/shard_map/ppermute | solution.py:282
  60.4 9.9 %copy-start.2 = (bf16[1,256,512]{2,1,0:T(8,128)(2,1)S(1)}, bf16[1,256,512]{2,1,0:T(8,128)(2,1)}, u32[]{:S(2)}) copy-start(bf16[1,256,512]{2,1,0:T(8,128)(2,1)} %copy-done.1) | copy-start | bytes 786436
  70.2 24.4 %copy-start.3 = (f32[256]{0:T(256)S(1)}, f32[256]{0:T(256)}, u32[]{:S(2)}) copy-start(f32[256]{0:T(256)} %param.10) | copy-start | bytes 3076
  70.7 7.6 %collective-permute-start.8 = (f32[4,256,128]{2,1,0:T(8,128)S(1)}, f32[4,256,128]{2,1,0:T(8,128)S(1)}, u32[]{:S(2)}, u32[]{:S(2)}) collective-permute-start(f32[4,256,128]{2,1,0:T(8,128)S(1)} %get-tuple-element.55), channel_id=1, source_target_pairs={{0,4},{4,0},{8,12},{12,8},{16,20},{20,16},{24,28},{28,24},{32,36},... | collective-permute-start | bytes 1572872 | tf_op jit(solution)/shard_map/ppermute | solution.py:289
  78.4 11.1 %collective-permute-start.10 = (f32[256,128]{1,0:T(8,128)S(1)}, f32[256,128]{1,0:T(8,128)S(1)}, u32[]{:S(2)}, u32[]{:S(2)}) collective-permute-start(f32[256,128]{1,0:T(8,128)S(1)} %get-tuple-element.58), channel_id=1, source_target_pairs={{0,2},{1,3},{2,0},{3,1},{4,6},{5,7},{6,4},{7,5},{8,10},{9,11},{10,... | collective-permute-start | bytes 393224 | tf_op jit(solution)/shard_map/ppermute | solution.py:293
  83.2 6.7 %collective-permute-start.11 = (f32[256,128]{1,0:T(8,128)S(1)}, f32[256,128]{1,0:T(8,128)S(1)}, u32[]{:S(2)}, u32[]{:S(2)}) collective-permute-start(f32[256,128]{1,0:T(8,128)S(1)} %get-tuple-element.59), channel_id=1, source_target_pairs={{0,1},{1,0},{2,3},{3,2},{4,5},{5,4},{6,7},{7,6},{8,9},{9,8},{10,11... | collective-permute-start | bytes 393224 | tf_op jit(solution)/shard_map/ppermute | solution.py:293
  85.3 9.3 %collective-permute-start.9 = (f32[256,128]{1,0:T(8,128)S(1)}, f32[256,128]{1,0:T(8,128)S(1)}, u32[]{:S(2)}, u32[]{:S(2)}) collective-permute-start(f32[256,128]{1,0:T(8,128)S(1)} %get-tuple-element.57), channel_id=1, source_target_pairs={{0,3},{1,2},{2,1},{3,0},{4,7},{5,6},{6,5},{7,4},{8,11},{9,10},{10,... | collective-permute-start | bytes 393224 | tf_op jit(solution)/shard_map/ppermute | solution.py:293

commit v5 on v4

--- a/solution.py
+++ b/solution.py
@@ -60,10 +60,10 @@
     ]
     for copy in fetch:
         copy.start()
-    for copy in fetch:
-        copy.wait()
+    fetch[1].wait()
     rows = amp_here.shape[1]
     hot = (lax.broadcasted_iota(jnp.int32, (rows, OCC), 0) == subset_here[...]).astype(jnp.bfloat16)
+    fetch[0].wait()
     shard_ref[...] = jnp.dot(amp_here[...], hot, preferred_element_type=jnp.float32).astype(jnp.bfloat16)
     copies = [
         pltpu.make_async_copy(shard_ref, copies_ref.at[pl.ds(copy * SHARD, SHARD), :], sems.at[copy])
@@ -248,8 +248,7 @@
         lax.all_to_all, axis_name="blk", split_axis=0, concat_axis=0, axis_index_groups=groups(), tiled=True
     )
     own = exchange(copies)
-    pair_irrep, ints, copies = lax.optimization_barrier((pair_irrep, ladder_ints, copies))
-    got = permute(ints, perm=across_core())
+    pair_irrep, copies = lax.optimization_barrier((pair_irrep, copies))
 
     t = jnp.arange(8, dtype=jnp.int32)
     z_from = [z, z - 1, z + 1, z - 2, z + 2, z + 4, z + 3, z - 3]
@@ -270,7 +269,8 @@
 
     own = lax.all_to_all(copies, "blk", 0, 0, axis_index_groups=groups(), tiled=True)
     near = prepare(place, ladder_ints.reshape(64, 2, SHARD, COLS), low[:, :COLS], high[:, :COLS])
-    own, near = lax.optimization_barrier((own, near))
+    own, near, ints = lax.optimization_barrier((own, near, ladder_ints))
+    got = permute(ints, perm=across_core())
     opposite = permute(own, perm=across())
     far = prepare(place, got.reshape(64, 2, SHARD, COLS), low[:, COLS:], high[:, COLS:])
     own_subset = lax.dynamic_slice_in_dim(pair_subset, me * OWN, OWN, 0)

time: 96.1 us -> 96.1 us (level)
    ppermute x1, starting transfers between devices: 8.79 us -> 2.25 us  [body(): got = permute(ints, perm=across_core())]
    all_to_all x1, starting transfers between devices: 4.67 us -> 10.9 us  [body(): lax.all_to_all(copies, 'blk', 0, 0, axis_index_groups=groups(), tiled=True)]
where the time goes in v5:
time: 96.1 us; the launch traced here: 95.5 us
  starting transfers between devices  55.8 us (58%)
  waiting for transfers between devices  23.1 us (24%)
  Pallas kernels  13.1 us (14%)
  local copies, waits for them, and re-layouts  2.12 us (2%)
    ppermute x3, starting transfers between devices, body(): lax.ppermute(dealt[step], 'grp', [(i, i ^ step) for i in range(GRP)])  10.9 us
    all_to_all x1, starting transfers between devices, body(): lax.all_to_all(copies, 'blk', 0, 0, axis_index_groups=groups(), tiled=True)  10.9 us
    ppermute x1, waiting for transfers between devices, body(): p3 = permute(opposite, perm=ring(1))  9.14 us
    ppermute x1, starting transfers between devices, body(): opposite = permute(own, perm=across())  7.45 us
    all_to_all x1, waiting for transfers between devices, body(): lax.all_to_all(copies, 'blk', 0, 0, axis_index_groups=groups(), tiled=True)  7.27 us
    ppermute x1, starting transfers between devices, body(): other = permute(away, perm=across_core())  6.64 us
    pallas_call x2, Pallas kernels, prepare(): pl.pallas_call(prepare_kernel, out_shape=[jax.ShapeDtypeStruct((len(numbe...  6.06 us
    ppermute x3, waiting for transfers between devices, body(): lax.ppermute(dealt[step], 'grp', [(i, i ^ step) for i in range(GRP)])  5.21 us
  transfers between devices with their start and end apart: 13, of which 5 were waited for; matrix products, arithmetic and copies ran while one was open for 2% of the time, Pallas kernels for 10%

profile of v5, /device:TPU:1, one launch (start us, length us, event | category | flops | bytes accessed | tf_op | source)
XLA Modules:
  0.0 95.5 jit_solution(10150743406143328369)
XLA Ops:
  0.0 0.0 copy-start
  0.0 0.0 copy-start.4
  0.0 2.3 %select.55 = bf16[512,512]{1,0:T(8,128)(2,1)} custom-call(bf16[64,1024]{1,0:T(8,128)(2,1)} %bitcast.21, s32[1,512]{1,0:T(1,128)} %bitcast.24), custom_call_target="tpu_custom_call" | custom-call | tf_op jit(solution)/shard_map/select/pallas_call | solution.py:80
  2.3 10.9 %all-to-all-start = ((bf16[8,64,512]{2,1,0:T(8,128)(2,1)}), bf16[8,64,512]{2,1,0:T(8,128)(2,1)S(1)}, u32[]{:S(2)}, u32[]{:S(2)}) async-start(bf16[8,64,512]{2,1,0:T(8,128)(2,1)} %bitcast.4), calls=%async_computation | async-start | bytes 1048576 | tf_op jit(solution)/shard_map/all_to_all | solution.py:270
  13.4 0.0 copy-done.4
  13.4 0.1 fusion.1
  13.5 0.1 concatenate.13
  13.6 0.1 concatenate.12
  13.6 0.1 pad_add_fusion.1.place_ref
  13.7 0.4 convert_reduce_fusion
  14.1 0.1 fusion.4
  14.2 0.1 select_reduce_fusion
  14.3 0.0 copy-start.5
  14.3 3.0 %prepare.2 = (bf16[3,256,512]{2,1,0:T(8,128)(2,1)S(1)}, bf16[2,256,512]{2,1,0:T(8,128)(2,1)S(1)}, bf16[2,256,512]{2,1,0:T(8,128)(2,1)S(1)}, bf16[1,256,512]{2,1,0:T(8,128)(2,1)S(1)}) custom-call(s32[66]{0:T(128)S(1)} %pad_add_fusion.1.place_ref, bf16[64,2,64,256]{3,2,1,0:T(8,128)(2,1)} %bitcast.20, s32[1,256]{1,0:T(1,128)S(1)} %get-tuple-element.87.low_ref, ...), custom_call_target="tpu_custom_call" | custom-call | bytes 6291456 | tf_op jit(solution)/shard_map/prepare/pallas_call | solution.py:140
  17.3 0.0 copy-start.1
  17.4 0.7 copy-done.1
  18.0 7.3 %all-to-all-done = bf16[8,64,512]{2,1,0:T(8,128)(2,1)S(1)} async-done(((bf16[8,64,512]{2,1,0:T(8,128)(2,1)}), bf16[8,64,512]{2,1,0:T(8,128)(2,1)S(1)}, u32[]{:S(2)}, u32[]{:S(2)}) %all-to-all-start) | async-done | bytes 524320 | tf_op jit(solution)/shard_map/all_to_all | solution.py:270
  25.3 2.2 %collective-permute-start.1 = (bf16[8192,256]{1,0:T(8,128)(2,1)}, bf16[8192,256]{1,0:T(8,128)(2,1)}, u32[]{:S(2)}, u32[]{:S(2)}) collective-permute-start(bf16[8192,256]{1,0:T(8,128)(2,1)} %param.7), channel_id=1, source_target_pairs={{0,4},{4,0},{8,12},{12,8},{16,20},{20,16},{24,28},{28,24},{32,36},... | collective-permute-start | bytes 12582920 | tf_op jit(solution)/shard_map/ppermute | solution.py:273
  27.6 2.8 %collective-permute-start.6 = (bf16[512,512]{1,0:T(8,128)(2,1)S(1)}, bf16[512,512]{1,0:T(8,128)(2,1)}, u32[]{:S(2)}, u32[]{:S(2)}) collective-permute-start(bf16[512,512]{1,0:T(8,128)(2,1)S(1)} %bitcast.15), channel_id=1, source_target_pairs={{0,32},{4,12},{8,40},{12,20},{16,48},{20,28},{24,56},{28,4},{32,64... | collective-permute-start | bytes 1572872 | tf_op jit(solution)/shard_map/ppermute | solution.py:279
  30.4 7.5 %collective-permute-start = (bf16[512,512]{1,0:T(8,128)(2,1)S(1)}, bf16[512,512]{1,0:T(8,128)(2,1)S(1)}, u32[]{:S(2)}, u32[]{:S(2)}) collective-permute-start(bf16[512,512]{1,0:T(8,128)(2,1)S(1)} %bitcast.16), channel_id=1, source_target_pairs={{0,128},{4,260},{8,136},{12,268},{16,144},{20,276},{24,152},{28,28... | collective-permute-start | bytes 1572872 | tf_op jit(solution)/shard_map/ppermute | solution.py:274
  37.8 3.4 %collective-permute-start.2 = (bf16[512,512]{1,0:T(8,128)(2,1)S(1)}, bf16[512,512]{1,0:T(8,128)(2,1)S(1)}, u32[]{:S(2)}, u32[]{:S(2)}) collective-permute-start(bf16[512,512]{1,0:T(8,128)(2,1)S(1)} %bitcast.17), channel_id=1, source_target_pairs={{0,224},{4,28},{8,232},{12,4},{16,240},{20,12},{24,248},{28,20},{3... | collective-permute-start | bytes 1572872 | tf_op jit(solution)/shard_map/ppermute | solution.py:280
  41.2 0.0 copy-done.5
  41.2 0.1 compare_select_fusion
  41.3 0.0 copy-done
  41.3 1.0 %gather_fusion = f32[128]{0:T(128)S(1)} fusion(f32[1024]{0:T(1024)S(1)} %copy-done, s32[1024]{0:T(1024)S(1)} %pad_clamp_fusion), kind=kCustom, calls=%fused_computation | custom fusion | bytes 1536 | tf_op jit(solution)/shard_map/jit(_take)/gather | solution.py:277
  42.3 0.0 collective-permute-done.6.refs_1_
  42.3 1.9 %collective-permute-start.7 = (bf16[512,512]{1,0:T(8,128)(2,1)}, bf16[512,512]{1,0:T(8,128)(2,1)S(1)}, u32[]{:S(2)}, u32[]{:S(2)}) collective-permute-start(bf16[512,512]{1,0:T(8,128)(2,1)} %collective-permute-done.6.refs_1_), channel_id=1, source_target_pairs={{0,32},{4,12},{8,40},{12,20},{16,48},{20,28},{24,56},{28,4},{32,64... | collective-permute-start | bytes 1572872 | tf_op jit(solution)/shard_map/ppermute | solution.py:281
  44.2 0.1 and_select_fusion
  44.3 0.0 collective-permute-done.1
  44.3 3.0 %prepare.3 = (bf16[3,256,512]{2,1,0:T(8,128)(2,1)S(1)}, bf16[2,256,512]{2,1,0:T(8,128)(2,1)S(1)}, bf16[2,256,512]{2,1,0:T(8,128)(2,1)S(1)}, bf16[1,256,512]{2,1,0:T(8,128)(2,1)S(1)}) custom-call(s32[66]{0:T(128)S(1)} %pad_add_fusion.1.place_ref, bf16[64,2,64,256]{3,2,1,0:T(8,128)(2,1)} %bitcast.11.ints_ref, s32[1,256]{1,0:T(1,128)S(1)} %get-tuple-element.88.low_ref, ...), custom_call_target="tpu_custom_call" | custom-call | bytes 6291456 | tf_op jit(solution)/shard_map/prepare/pallas_call | solution.py:140
  47.4 0.0 collective-permute-done.second_ref.refs_1_
  47.4 4.6 %collective-permute-start.4 = (bf16[512,512]{1,0:T(8,128)(2,1)S(1)}, bf16[512,512]{1,0:T(8,128)(2,1)S(1)}, u32[]{:S(2)}, u32[]{:S(2)}) collective-permute-start(bf16[512,512]{1,0:T(8,128)(2,1)S(1)} %collective-permute-done.second_ref.refs_1_), channel_id=1, source_target_pairs={{0,224},{4,28},{8,232},{12,4},{16,240},{20,12},{24,248},{28,20},{3... | collective-permute-start | bytes 1572872 | tf_op jit(solution)/shard_map/ppermute | solution.py:283
  51.9 1.9 %collective-permute-start.5 = (bf16[512,512]{1,0:T(8,128)(2,1)S(1)}, bf16[512,512]{1,0:T(8,128)(2,1)S(1)}, u32[]{:S(2)}, u32[]{:S(2)}) collective-permute-start(bf16[512,512]{1,0:T(8,128)(2,1)S(1)} %collective-permute-done.second_ref.refs_1_), channel_id=1, source_target_pairs={{0,32},{4,12},{8,40},{12,20},{16,48},{20,28},{24,56},{28,4},{32,64... | collective-permute-start | bytes 1572872 | tf_op jit(solution)/shard_map/ppermute | solution.py:284
  53.9 0.0 collective-permute-done.2.first_ref.refs_2_
  53.9 3.1 %collective-permute-start.3 = (bf16[512,512]{1,0:T(8,128)(2,1)S(1)}, bf16[512,512]{1,0:T(8,128)(2,1)S(1)}, u32[]{:S(2)}, u32[]{:S(2)}) collective-permute-start(bf16[512,512]{1,0:T(8,128)(2,1)S(1)} %pick.1), channel_id=1, source_target_pairs={{0,224},{8,232},{16,240},{24,248},{32,0},{40,8},{48,16},{56,24},{6... | collective-permute-start | bytes 1572872 | tf_op jit(solution)/shard_map/ppermute | solution.py:282
  57.1 2.0 %early.3.refs_2_ = f32[512,512]{1,0:T(8,128)S(1)} custom-call(bf16[3,256,512]{2,1,0:T(8,128)(2,1)S(1)} %get-tuple-element.52.near_ref, bf16[3,256,512]{2,1,0:T(8,128)(2,1)S(1)} %get-tuple-element.53.far_ref, bf16[512,512]{1,0:T(8,128)(2,1)S(1)} %bitcast.18, bf16[512,512]{1,0:T(8,128)(2,1)} %collective-permute-done.6.refs_1_, ...), custom_call_target="tpu_custom_call" | custom-call | flops 805306368 | bytes 3145728 | tf_op jit(solution)/shard_map/early/pallas_call | solution.py:166
  59.1 0.0 collective-permute-done.7.refs_0_
  59.1 0.7 early.4.refs_2_
  59.8 0.0 copy-start.2
  59.8 0.0 collective-permute-done.4.refs_0_
  59.9 9.1 %collective-permute-done.5.refs_1_ = bf16[512,512]{1,0:T(8,128)(2,1)S(1)} collective-permute-done((bf16[512,512]{1,0:T(8,128)(2,1)S(1)}, bf16[512,512]{1,0:T(8,128)(2,1)S(1)}, u32[]{:S(2)}, u32[]{:S(2)}) %collective-permute-start.5) | collective-permute-done | bytes 524320 | tf_op jit(solution)/shard_map/ppermute | solution.py:284
  69.0 0.7 early.5.before_ref
  69.7 0.0 copy-start.3
  69.7 0.0 collective-permute-done.3.piece_ref
  69.7 0.0 copy-done.2
  69.7 0.4 tail.1
  70.2 6.6 %collective-permute-start.8 = (f32[4,256,128]{2,1,0:T(8,128)S(1)}, f32[4,256,128]{2,1,0:T(8,128)S(1)}, u32[]{:S(2)}, u32[]{:S(2)}) collective-permute-start(f32[4,256,128]{2,1,0:T(8,128)S(1)} %get-tuple-element.55), channel_id=1, source_target_pairs={{0,4},{4,0},{8,12},{12,8},{16,20},{20,16},{24,28},{28,24},{32,36},... | collective-permute-start | bytes 1572872 | tf_op jit(solution)/shard_map/ppermute | solution.py:289
  76.8 1.5 %collective-permute-done.8.other_ref = f32[4,256,128]{2,1,0:T(8,128)S(1)} collective-permute-done((f32[4,256,128]{2,1,0:T(8,128)S(1)}, f32[4,256,128]{2,1,0:T(8,128)S(1)}, u32[]{:S(2)}, u32[]{:S(2)}) %collective-permute-start.8) | collective-permute-done | bytes 524320 | tf_op jit(solution)/shard_map/ppermute | solution.py:289
  78.3 0.1 deal.1
  78.4 4.8 %collective-permute-start.10 = (f32[256,128]{1,0:T(8,128)S(1)}, f32[256,128]{1,0:T(8,128)S(1)}, u32[]{:S(2)}, u32[]{:S(2)}) collective-permute-start(f32[256,128]{1,0:T(8,128)S(1)} %get-tuple-element.58), channel_id=1, source_target_pairs={{0,2},{1,3},{2,0},{3,1},{4,6},{5,7},{6,4},{7,5},{8,10},{9,11},{10,... | collective-permute-start | bytes 393224 | tf_op jit(solution)/shard_map/ppermute | solution.py:293
  83.2 2.1 %collective-permute-start.11 = (f32[256,128]{1,0:T(8,128)S(1)}, f32[256,128]{1,0:T(8,128)S(1)}, u32[]{:S(2)}, u32[]{:S(2)}) collective-permute-start(f32[256,128]{1,0:T(8,128)S(1)} %get-tuple-element.59), channel_id=1, source_target_pairs={{0,1},{1,0},{2,3},{3,2},{4,5},{5,4},{6,7},{7,6},{8,9},{9,8},{10,11... | collective-permute-start | bytes 393224 | tf_op jit(solution)/shard_map/ppermute | solution.py:293
  85.4 4.0 %collective-permute-start.9 = (f32[256,128]{1,0:T(8,128)S(1)}, f32[256,128]{1,0:T(8,128)S(1)}, u32[]{:S(2)}, u32[]{:S(2)}) collective-permute-start(f32[256,128]{1,0:T(8,128)S(1)} %get-tuple-element.57), channel_id=1, source_target_pairs={{0,3},{1,2},{2,1},{3,0},{4,7},{5,6},{6,5},{7,4},{8,11},{9,10},{10,... | collective-permute-start | bytes 393224 | tf_op jit(solution)/shard_map/ppermute | solution.py:293
  89.3 0.1 copy.9.gap_ref
  89.5 0.0 collective-permute-done.10.c_ref
  89.5 0.6 collective-permute-done.11.d_ref
  90.0 4.6 %collective-permute-done.9.b_ref = f32[256,128]{1,0:T(8,128)S(1)} collective-permute-done((f32[256,128]{1,0:T(8,128)S(1)}, f32[256,128]{1,0:T(8,128)S(1)}, u32[]{:S(2)}, u32[]{:S(2)}) %collective-permute-start.9) | collective-permute-done | bytes 131104 | tf_op jit(solution)/shard_map/ppermute | solution.py:293
  94.7 0.0 copy-done.3
  94.7 0.8 close.1
  (13 shorter events, 0.1 us)
Async XLA Ops:
  0.0 41.3 %copy-start = (f32[1024]{0:T(1024)S(1)}, f32[1024]{0:T(1024)}, u32[]{:S(2)}) copy-start(f32[1024]{0:T(1024)} %param.9) | copy-start | bytes 12292
  0.0 13.4 %copy-start.4 = (s32[32768]{0:T(1024)S(1)}, s32[32768]{0:T(1024)}, u32[]{:S(2)}) copy-start(s32[32768]{0:T(1024)} %param.8) | copy-start | bytes 393220
  2.3 23.0 %all-to-all-start = ((bf16[8,64,512]{2,1,0:T(8,128)(2,1)}), bf16[8,64,512]{2,1,0:T(8,128)(2,1)S(1)}, u32[]{:S(2)}, u32[]{:S(2)}) async-start(bf16[8,64,512]{2,1,0:T(8,128)(2,1)} %bitcast.4), calls=%async_computation | async-start | bytes 1048576 | tf_op jit(solution)/shard_map/all_to_all | solution.py:270
  14.3 26.9 %copy-start.5 = (s32[512]{0:T(512)S(1)}, s32[512]{0:T(512)}, u32[]{:S(2)}) copy-start(s32[512]{0:T(512)} %param.11) | copy-start | bytes 6148
  17.3 0.7 copy-start.1
  25.3 19.0 %collective-permute-start.1 = (bf16[8192,256]{1,0:T(8,128)(2,1)}, bf16[8192,256]{1,0:T(8,128)(2,1)}, u32[]{:S(2)}, u32[]{:S(2)}) collective-permute-start(bf16[8192,256]{1,0:T(8,128)(2,1)} %param.7), channel_id=1, source_target_pairs={{0,4},{4,0},{8,12},{12,8},{16,20},{20,16},{24,28},{28,24},{32,36},... | collective-permute-start | bytes 12582920 | tf_op jit(solution)/shard_map/ppermute | solution.py:273
  27.6 14.7 %collective-permute-start.6 = (bf16[512,512]{1,0:T(8,128)(2,1)S(1)}, bf16[512,512]{1,0:T(8,128)(2,1)}, u32[]{:S(2)}, u32[]{:S(2)}) collective-permute-start(bf16[512,512]{1,0:T(8,128)(2,1)S(1)} %bitcast.15), channel_id=1, source_target_pairs={{0,32},{4,12},{8,40},{12,20},{16,48},{20,28},{24,56},{28,4},{32,64... | collective-permute-start | bytes 1572872 | tf_op jit(solution)/shard_map/ppermute | solution.py:279
  30.4 17.0 %collective-permute-start = (bf16[512,512]{1,0:T(8,128)(2,1)S(1)}, bf16[512,512]{1,0:T(8,128)(2,1)S(1)}, u32[]{:S(2)}, u32[]{:S(2)}) collective-permute-start(bf16[512,512]{1,0:T(8,128)(2,1)S(1)} %bitcast.16), channel_id=1, source_target_pairs={{0,128},{4,260},{8,136},{12,268},{16,144},{20,276},{24,152},{28,28... | collective-permute-start | bytes 1572872 | tf_op jit(solution)/shard_map/ppermute | solution.py:274
  37.8 16.0 %collective-permute-start.2 = (bf16[512,512]{1,0:T(8,128)(2,1)S(1)}, bf16[512,512]{1,0:T(8,128)(2,1)S(1)}, u32[]{:S(2)}, u32[]{:S(2)}) collective-permute-start(bf16[512,512]{1,0:T(8,128)(2,1)S(1)} %bitcast.17), channel_id=1, source_target_pairs={{0,224},{4,28},{8,232},{12,4},{16,240},{20,12},{24,248},{28,20},{3... | collective-permute-start | bytes 1572872 | tf_op jit(solution)/shard_map/ppermute | solution.py:280
  42.3 16.8 %collective-permute-start.7 = (bf16[512,512]{1,0:T(8,128)(2,1)}, bf16[512,512]{1,0:T(8,128)(2,1)S(1)}, u32[]{:S(2)}, u32[]{:S(2)}) collective-permute-start(bf16[512,512]{1,0:T(8,128)(2,1)} %collective-permute-done.6.refs_1_), channel_id=1, source_target_pairs={{0,32},{4,12},{8,40},{12,20},{16,48},{20,28},{24,56},{28,4},{32,64... | collective-permute-start | bytes 1572872 | tf_op jit(solution)/shard_map/ppermute | solution.py:281
  47.4 12.5 %collective-permute-start.4 = (bf16[512,512]{1,0:T(8,128)(2,1)S(1)}, bf16[512,512]{1,0:T(8,128)(2,1)S(1)}, u32[]{:S(2)}, u32[]{:S(2)}) collective-permute-start(bf16[512,512]{1,0:T(8,128)(2,1)S(1)} %collective-permute-done.second_ref.refs_1_), channel_id=1, source_target_pairs={{0,224},{4,28},{8,232},{12,4},{16,240},{20,12},{24,248},{28,20},{3... | collective-permute-start | bytes 1572872 | tf_op jit(solution)/shard_map/ppermute | solution.py:283
  51.9 17.0 %collective-permute-start.5 = (bf16[512,512]{1,0:T(8,128)(2,1)S(1)}, bf16[512,512]{1,0:T(8,128)(2,1)S(1)}, u32[]{:S(2)}, u32[]{:S(2)}) collective-permute-start(bf16[512,512]{1,0:T(8,128)(2,1)S(1)} %collective-permute-done.second_ref.refs_1_), channel_id=1, source_target_pairs={{0,32},{4,12},{8,40},{12,20},{16,48},{20,28},{24,56},{28,4},{32,64... | collective-permute-start | bytes 1572872 | tf_op jit(solution)/shard_map/ppermute | solution.py:284
  53.9 15.8 %collective-permute-start.3 = (bf16[512,512]{1,0:T(8,128)(2,1)S(1)}, bf16[512,512]{1,0:T(8,128)(2,1)S(1)}, u32[]{:S(2)}, u32[]{:S(2)}) collective-permute-start(bf16[512,512]{1,0:T(8,128)(2,1)S(1)} %pick.1), channel_id=1, source_target_pairs={{0,224},{8,232},{16,240},{24,248},{32,0},{40,8},{48,16},{56,24},{6... | collective-permute-start | bytes 1572872 | tf_op jit(solution)/shard_map/ppermute | solution.py:282
  59.8 9.9 %copy-start.2 = (bf16[1,256,512]{2,1,0:T(8,128)(2,1)S(1)}, bf16[1,256,512]{2,1,0:T(8,128)(2,1)}, u32[]{:S(2)}) copy-start(bf16[1,256,512]{2,1,0:T(8,128)(2,1)} %copy-done.1) | copy-start | bytes 786436
  69.7 25.0 %copy-start.3 = (f32[256]{0:T(256)S(1)}, f32[256]{0:T(256)}, u32[]{:S(2)}) copy-start(f32[256]{0:T(256)} %param.10) | copy-start | bytes 3076
  70.2 8.2 %collective-permute-start.8 = (f32[4,256,128]{2,1,0:T(8,128)S(1)}, f32[4,256,128]{2,1,0:T(8,128)S(1)}, u32[]{:S(2)}, u32[]{:S(2)}) collective-permute-start(f32[4,256,128]{2,1,0:T(8,128)S(1)} %get-tuple-element.55), channel_id=1, source_target_pairs={{0,4},{4,0},{8,12},{12,8},{16,20},{20,16},{24,28},{28,24},{32,36},... | collective-permute-start | bytes 1572872 | tf_op jit(solution)/shard_map/ppermute | solution.py:289
  78.4 11.1 %collective-permute-start.10 = (f32[256,128]{1,0:T(8,128)S(1)}, f32[256,128]{1,0:T(8,128)S(1)}, u32[]{:S(2)}, u32[]{:S(2)}) collective-permute-start(f32[256,128]{1,0:T(8,128)S(1)} %get-tuple-element.58), channel_id=1, source_target_pairs={{0,2},{1,3},{2,0},{3,1},{4,6},{5,7},{6,4},{7,5},{8,10},{9,11},{10,... | collective-permute-start | bytes 393224 | tf_op jit(solution)/shard_map/ppermute | solution.py:293
  83.2 6.8 %collective-permute-start.11 = (f32[256,128]{1,0:T(8,128)S(1)}, f32[256,128]{1,0:T(8,128)S(1)}, u32[]{:S(2)}, u32[]{:S(2)}) collective-permute-start(f32[256,128]{1,0:T(8,128)S(1)} %get-tuple-element.59), channel_id=1, source_target_pairs={{0,1},{1,0},{2,3},{3,2},{4,5},{5,4},{6,7},{7,6},{8,9},{9,8},{10,11... | collective-permute-start | bytes 393224 | tf_op jit(solution)/shard_map/ppermute | solution.py:293
  85.4 9.3 %collective-permute-start.9 = (f32[256,128]{1,0:T(8,128)S(1)}, f32[256,128]{1,0:T(8,128)S(1)}, u32[]{:S(2)}, u32[]{:S(2)}) collective-permute-start(f32[256,128]{1,0:T(8,128)S(1)} %get-tuple-element.57), channel_id=1, source_target_pairs={{0,3},{1,2},{2,1},{3,0},{4,7},{5,6},{6,5},{7,4},{8,11},{9,10},{10,... | collective-permute-start | bytes 393224 | tf_op jit(solution)/shard_map/ppermute | solution.py:293
